TPU v7x, 256 devices: a whole 4x4x8 slice. The times are simulated.
256 devices in a mesh: section: 16 (over z, x_hi), tensor: 8 (over x_lo, y), dp: 2 (over core).
Axes of the slice: x: 4 (x_hi: 2, x_lo: 2; x = x_hi * 2 + x_lo), y: 4, z: 8, core: 2. Of those that a mesh axis runs over, the one named last changes fastest.
Arguments:
- base_weight: bfloat16 [16, 8192, 8192], P('section', ('tensor', 'dp')), may hold values from -0.0625 to 0.0625
- pol_down: bfloat16 [16, 8192, 128], P('section', ('tensor', 'dp')), may hold values from -0.0625 to 0.0625
- pol_up: bfloat16 [16, 128, 8192], P('section', None, ('tensor', 'dp')), may hold values from -0.5 to 0.5
- old_down: bfloat16 [16, 8192, 128], P('section', ('tensor', 'dp')), may hold values from -0.0625 to 0.0625
- old_up: bfloat16 [16, 128, 8192], P('section', None, ('tensor', 'dp')), may hold values from -0.5 to 0.5
- pol_in: bfloat16 [16, 256, 8192], P('section', 'dp', 'tensor'), may hold values from -6 to 6
- ref_in: bfloat16 [16, 256, 8192], P('section', 'dp', 'tensor'), may hold values from -6 to 6
- grad_in: bfloat16 [16, 256, 8192], P('section', 'dp', 'tensor'), may hold values from -6 to 6
- stash: bfloat16 [16, 2, 256, 8192], P('section', None, 'dp', 'tensor'), may hold values from -6 to 6
- fresh_pol: bfloat16 [1, 256, 8192], P(None, 'dp', 'tensor'), may hold values from -6 to 6
- fresh_ref: bfloat16 [1, 256, 8192], P(None, 'dp', 'tensor'), may hold values from -6 to 6
- targets: bfloat16 [2, 256, 8192], P(None, 'dp', 'tensor'), may hold values from -1 to 1
- final_gain: float32 [8192], P('tensor'), may hold values from 0.5 to 1.5
- token_side: int32 [2, 256], P(None, 'dp'), may hold values from 0 to 2, as said below
- ref_logratio: float32 [2, 2], P(None, 'dp'), may hold values from -32 to 32
Outputs:
- pol_out: bfloat16 [16, 256, 8192], P('section', 'dp', 'tensor')
- ref_out: bfloat16 [16, 256, 8192], P('section', 'dp', 'tensor')
- grad_out: bfloat16 [16, 256, 8192], P('section', 'dp', 'tensor')
- grad_down: float32 [16, 8192, 128], P('section', ('tensor', 'dp'))
- grad_up: float32 [16, 128, 8192], P('section', None, ('tensor', 'dp'))
Inputs may be any that keep to these rules, and one draw needn't show every extreme that they name: `token_side`: 0 marks padding, 1 a token of the chosen answer, 2 a token of the rejected answer; within the rows of a pair the 1s are a leading run of the first half of its 128 rows and the 2s a leading run of the second half, each run of even length from 2 to half of 128, and one of the two runs fills its half.
All inputs are finite; a program needn't handle non-finite values.
Results may differ from a plain program's by a relative error of at most 0.01.
Values may be sent and summed in bfloat16 or wider, within the bound.
A program may use at most 128 MiB of HBM per device.

v0:
```python
import jax
import jax.numpy as jnp
from jax import lax
from jax.sharding import PartitionSpec as P

D = 8192
TICKS = 2


ADAPTER_SCALE = 0.5
MIX_WEIGHT = 0.6
PREF_BETA = 0.1
LOSS_SCALE = 1024.0
NORM_EPSILON = 1e-06


def passed_along(block, axis, distance):
    devices = range(lax.axis_size(axis))
    route = [(i - distance, i) for i in devices if i - distance in devices]
    return lax.ppermute(block, axis, route)


def mixed(first, second):
    return (
        MIX_WEIGHT * first.astype(jnp.float32) + (1.0 - MIX_WEIGHT) * second.astype(jnp.float32)
    ).astype(jnp.bfloat16)


def finish_layer(layer_activation, frozen_weight, adapter_product, up_weight):
    combined_output = (
        layer_activation.astype(jnp.float32)
        + frozen_weight
        + ADAPTER_SCALE
        * jnp.dot(
            adapter_product.astype(jnp.bfloat16), up_weight, preferred_element_type=jnp.float32
        )
    )
    return combined_output.astype(jnp.bfloat16)


def head_cotangent(hidden, target, gain, side, ref_ratio):
    hidden_f = hidden.astype(jnp.float32)
    target_f = target.astype(jnp.float32)
    sumsq, inner = lax.psum(
        (jnp.sum(hidden_f * hidden_f, axis=-1), jnp.sum(hidden_f * gain * target_f, axis=-1)),
        "tensor",
    )
    inv_rms = lax.rsqrt(sumsq / D + NORM_EPSILON)
    sign = (side == 1).astype(jnp.float32) - (side == 2).astype(jnp.float32)
    diff = jnp.sum(inner * inv_rms * sign)
    margin = PREF_BETA * (diff - ref_ratio[0])
    token_weight = -LOSS_SCALE * PREF_BETA * jax.nn.sigmoid(-margin) * sign
    incoming_gradient = token_weight[:, None] * (
        inv_rms[:, None] * gain * target_f - (inner * inv_rms**3 / D)[:, None] * hidden_f
    )
    return incoming_gradient.astype(jnp.bfloat16)


def on_device(
    base_weight,
    pol_down,
    pol_up,
    old_down,
    old_up,
    pol_in,
    ref_in,
    grad_in,
    stash,
    fresh_pol,
    fresh_ref,
    targets,
    final_gain,
    token_side,
    ref_logratio,
):
    sections = lax.axis_size("section")
    section_index = lax.axis_index("section")
    is_last = section_index == sections - 1
    is_first = section_index == 0
    weight = base_weight[0]
    policy_down = pol_down[0]
    up_pol = pol_up[0]
    down_ref = mixed(pol_down[0], old_down[0])
    up_ref = mixed(pol_up[0], old_up[0])
    pol_act = pol_in[0]
    ref_act = ref_in[0]
    cotan_in = grad_in[0]
    down_total = jnp.zeros(policy_down.shape, jnp.float32)
    up_total = jnp.zeros(up_pol.shape, jnp.float32)
    for tick_index in range(TICKS):
        pol_rows = lax.all_to_all(pol_act, "dp", split_axis=1, concat_axis=0, tiled=True)
        ref_rows = lax.all_to_all(ref_act, "dp", split_axis=1, concat_axis=0, tiled=True)
        low_pol, low_ref = lax.psum(
            (
                jnp.dot(pol_rows, policy_down, preferred_element_type=jnp.float32),
                jnp.dot(ref_rows, down_ref, preferred_element_type=jnp.float32),
            ),
            ("tensor", "dp"),
        )
        base_pol = lax.psum_scatter(
            jnp.dot(pol_rows, weight, preferred_element_type=jnp.float32),
            ("tensor", "dp"),
            scatter_dimension=1,
            tiled=True,
        )
        base_ref = lax.psum_scatter(
            jnp.dot(ref_rows, weight, preferred_element_type=jnp.float32),
            ("tensor", "dp"),
            scatter_dimension=1,
            tiled=True,
        )
        out_pol = finish_layer(pol_rows, base_pol, low_pol, up_pol)
        out_ref = finish_layer(ref_rows, base_ref, low_ref, up_ref)
        pol_next = lax.all_to_all(out_pol, "dp", split_axis=0, concat_axis=1, tiled=True)
        ref_next = lax.all_to_all(out_ref, "dp", split_axis=0, concat_axis=1, tiled=True)
        head_cot = head_cotangent(
            pol_next,
            targets[tick_index],
            final_gain,
            token_side[tick_index],
            ref_logratio[tick_index],
        )
        incoming_gradient = jnp.where(is_last, head_cot, cotan_in)
        stored_input = jnp.where(is_last, pol_act, stash[0, tick_index])
        gradient_rows = lax.all_to_all(
            incoming_gradient, "dp", split_axis=1, concat_axis=0, tiled=True
        )
        stored_rows = lax.all_to_all(stored_input, "dp", split_axis=1, concat_axis=0, tiled=True)
        adapter_product, backward_signal = lax.psum(
            (
                jnp.dot(stored_rows, policy_down, preferred_element_type=jnp.float32),
                jnp.dot(gradient_rows, up_pol.T, preferred_element_type=jnp.float32),
            ),
            ("tensor", "dp"),
        )
        through = jnp.dot(
            lax.all_gather(gradient_rows, ("tensor", "dp"), axis=1, tiled=True),
            weight.T,
            preferred_element_type=jnp.float32,
        )
        adapter_product = adapter_product.astype(jnp.bfloat16)
        backward_signal = backward_signal.astype(jnp.bfloat16)
        combined_output = (
            gradient_rows.astype(jnp.float32)
            + through
            + ADAPTER_SCALE
            * jnp.dot(backward_signal, policy_down.T, preferred_element_type=jnp.float32)
        )
        result = combined_output.astype(jnp.bfloat16)
        down_gradient = ADAPTER_SCALE * jnp.dot(
            stored_rows.T, backward_signal, preferred_element_type=jnp.float32
        )
        up_gradient = ADAPTER_SCALE * jnp.dot(
            adapter_product.T, gradient_rows, preferred_element_type=jnp.float32
        )
        result = lax.all_to_all(result, "dp", split_axis=0, concat_axis=1, tiled=True)
        back_next, down_gradient, up_gradient = (result, down_gradient, up_gradient)
        down_total = down_total + down_gradient
        up_total = up_total + up_gradient
        if tick_index + 1 < TICKS:
            moved_pol, moved_ref = passed_along((pol_next, ref_next), "section", 1)
            pol_act = jnp.where(is_first, fresh_pol[tick_index], moved_pol)
            ref_act = jnp.where(is_first, fresh_ref[tick_index], moved_ref)
            cotan_in = passed_along(back_next, "section", -1)
    return (pol_next[None], ref_next[None], back_next[None], down_total[None], up_total[None])


def solution(mesh):
    in_specs = (
        P("section", ("tensor", "dp"), None),
        P("section", ("tensor", "dp"), None),
        P("section", None, ("tensor", "dp")),
        P("section", ("tensor", "dp"), None),
        P("section", None, ("tensor", "dp")),
        P("section", "dp", "tensor"),
        P("section", "dp", "tensor"),
        P("section", "dp", "tensor"),
        P("section", None, "dp", "tensor"),
        P(None, "dp", "tensor"),
        P(None, "dp", "tensor"),
        P(None, "dp", "tensor"),
        P("tensor"),
        P(None, "dp"),
        P(None, "dp"),
    )
    out_specs = (
        P("section", "dp", "tensor"),
        P("section", "dp", "tensor"),
        P("section", "dp", "tensor"),
        P("section", ("tensor", "dp"), None),
        P("section", None, ("tensor", "dp")),
    )
    return jax.shard_map(
        on_device, mesh=mesh, in_specs=in_specs, out_specs=out_specs, check_vma=False
    )
```

profile of v0, /device:TPU:229, one launch (start us, length us, event | category | flops | bytes accessed | tf_op | source)
XLA Modules:
  0.0 499.5 jit_solution(9528255936709345866)
XLA Ops:
  7.2 1.1 fusion.96
  8.5 1.2 all_to_all.186
  9.7 4.3 all_to_all.251
  14.0 9.0 %fusion.10 = f32[256,8192]{1,0:T(8,128)} fusion(bf16[256,512]{1,0:T(8,128)(2,1)S(1)} %bitcast.178, bf16[1,512,8192]{2,1,0:T(8,128)(2,1)} %param.15), kind=kOutput, calls=%fused_computation.10 | convolution fusion | flops 2147483648 | bytes 17039360 | tf_op jit(solution)/shard_map/dot_general | solution.py:101
  23.0 0.8 copy-done
  24.0 53.8 %all-reduce.7 = bf16[256,128]{1,0:T(8,128)(2,1)S(1)} all-reduce(f32[256,128]{1,0:T(8,128)S(1)} %fusion.61), channel_id=1, replica_groups=mesh['section'=16,'tensor'=8,'dp'=2] {'tensor','dp'}, use_global_device_ids=true, to_apply=%region_1.0 | all-reduce | flops 32768 | bytes 196608 | tf_op jit(solution)/shard_map/psum | solution.py:93
  77.8 18.8 %reduce-scatter.5.cloned.1.call-done = f32[256,512]{1,0:T(8,128)} async-done(((f32[256,8192]{1,0:T(8,128)}), f32[256,512]{1,0:T(8,128)}) %reduce-scatter.5.cloned.1.call-update) | async-done | bytes 524304 | tf_op jit(solution)/shard_map/reduce_scatter | solution.py:100
  96.7 1.2 fusion.29
  97.9 8.0 %all_to_all.252 = bf16[2,128,512]{2,1,0:T(8,128)(2,1)S(1)} all-to-all(bf16[2,128,512]{2,1,0:T(8,128)(2,1)S(1)} %bitcast.203), channel_id=1, replica_groups=mesh['section'=16,'tensor'=8,'dp'=2] {'dp'}, dimensions={0} | all-to-all | bytes 524288 | tf_op jit(solution)/shard_map/all_to_all | solution.py:114
  106.1 1.3 collective-permute-start
  107.8 9.3 %collective-permute-done = bf16[128,1024]{0,1:T(8,128)(2,1)S(1)} collective-permute-done((bf16[128,1024]{0,1:T(8,128)(2,1)S(1)}, bf16[128,1024]{0,1:T(8,128)(2,1)S(1)}, u32[]{:S(2)}, u32[]{:S(2)}) %collective-permute-start) | collective-permute-done | bytes 262176 | tf_op jit(solution)/shard_map/ppermute | solution.py:20
  117.3 4.8 all_to_all.253
  122.0 9.0 %fusion.8 = f32[256,8192]{1,0:T(8,128)} fusion(bf16[256,512]{1,0:T(8,128)(2,1)S(1)} %bitcast.175, bf16[1,512,8192]{2,1,0:T(8,128)(2,1)} %param.15), kind=kOutput, calls=%fused_computation.8 | convolution fusion | flops 2147483648 | bytes 17039360 | tf_op jit(solution)/shard_map/dot_general | solution.py:101
  131.1 1.0 copy-done.5
  132.4 0.4 reshape.152
  132.9 1.2 squeeze.39
  134.1 0.6 fusion.98
  134.9 50.4 %all-reduce.8 = bf16[256,128]{1,0:T(8,128)(2,1)S(1)} all-reduce(f32[256,128]{1,0:T(8,128)S(1)} %fusion.59), channel_id=1, replica_groups=mesh['section'=16,'tensor'=8,'dp'=2] {'tensor','dp'}, use_global_device_ids=true, to_apply=%region_3.0 | all-reduce | flops 32768 | bytes 196608 | tf_op jit(solution)/shard_map/psum | solution.py:93
  185.3 18.7 %reduce-scatter.7.cloned.1.call-done = f32[256,512]{1,0:T(8,128)} async-done(((f32[256,8192]{1,0:T(8,128)}), f32[256,512]{1,0:T(8,128)}) %reduce-scatter.7.cloned.1.call-update) | async-done | bytes 524304 | tf_op jit(solution)/shard_map/reduce_scatter | solution.py:100
  204.0 1.3 fusion.28
  205.3 7.3 %all_to_all.254 = bf16[2,128,512]{2,1,0:T(8,128)(2,1)S(1)} all-to-all(bf16[2,128,512]{2,1,0:T(8,128)(2,1)S(1)} %bitcast.204), channel_id=1, replica_groups=mesh['section'=16,'tensor'=8,'dp'=2] {'dp'}, dimensions={0} | all-to-all | bytes 524288 | tf_op jit(solution)/shard_map/all_to_all | solution.py:114
  212.6 0.3 multiply_reduce_fusion
  212.9 13.5 %all-reduce.2 = (f32[128]{0:T(128)S(1)}, f32[128]{0:T(128)S(1)}, f32[128]{0:T(128)S(1)}, f32[128]{0:T(128)S(1)}) all-reduce(f32[128]{0:T(128)S(1)} %get-tuple-element.29, f32[128]{0:T(128)S(1)} %get-tuple-element.30, f32[128]{0:T(128)S(1)} %get-tuple-element.6, ...), channel_id=1, replica_groups=mesh['section'=16,'tensor'=8,'dp'=2] {'tensor'}, use_global_device_ids=true, to_apply=%region_14.15 | all-reduce | flops 512 | bytes 4096 | tf_op jit(solution)/shard_map/psum | solution.py:44
  226.3 0.6 multiply_reduce_fusion.3
  229.7 0.3 fusion.44
  230.1 8.4 %all_to_all.255 = bf16[128,2,512]{2,0,1:T(8,128)(2,1)} all-to-all(bf16[128,2,512]{2,0,1:T(8,128)(2,1)S(1)} %fusion.44), channel_id=1, replica_groups=mesh['section'=16,'tensor'=8,'dp'=2] {'dp'}, dimensions={1} | all-to-all | bytes 524288 | tf_op jit(solution)/shard_map/all_to_all | solution.py:125
  238.6 1.2 all_to_all.201
  239.8 3.9 all_to_all.256
  243.7 9.0 %fusion.6 = f32[256,8192]{1,0:T(8,128)} fusion(bf16[256,512]{1,0:T(8,128)(2,1)S(1)} %bitcast.181, bf16[1,512,8192]{2,1,0:T(8,128)(2,1)} %param.15), kind=kOutput, calls=%fused_computation.6 | convolution fusion | flops 2147483648 | bytes 17039360 | tf_op jit(solution)/shard_map/dot_general | solution.py:107
  252.7 0.8 copy-done.4
  253.6 0.2 convolution_bitcast_fusion
  254.0 53.2 %all-reduce.9 = (bf16[256,128]{0,1:T(8,128)(2,1)S(1)}, bf16[256,128]{1,0:T(8,128)(2,1)S(1)}) all-reduce(f32[256,128]{0,1:T(8,128)S(1)} %convolution_bitcast_fusion, f32[256,128]{1,0:T(8,128)S(1)} %fusion.49), channel_id=1, replica_groups=mesh['section'=16,'tensor'=8,'dp'=2] {'tensor','dp'}, use_global_device_ids=true, to_apply=%region_5.0 | all-reduce | flops 65536 | bytes 393216 | tf_op jit(solution)/shard_map/psum | solution.py:93
  307.3 7.3 %fusion.18 = f32[256,512]{1,0:T(8,128)S(1)} fusion(bf16[256,8192]{1,0:T(8,128)(2,1)} %all-gather.3.cloned.1.call-done, bf16[1,512,8192]{2,1,0:T(8,128)(2,1)} %param.15, bf16[256,512]{1,0:T(8,128)(2,1)S(1)} %bitcast.190), kind=kOutput, calls=%fused_computation.24 | convolution fusion | flops 2147745792 | bytes 13369344 | tf_op jit(solution)/shard_map/dot_general | solution.py:136
  314.9 7.4 %all_to_all.257 = bf16[2,128,512]{2,1,0:T(8,128)(2,1)S(1)} all-to-all(bf16[2,128,512]{2,1,0:T(8,128)(2,1)S(1)} %bitcast.216), channel_id=1, replica_groups=mesh['section'=16,'tensor'=8,'dp'=2] {'dp'}, dimensions={0} | all-to-all | bytes 524288 | tf_op jit(solution)/shard_map/all_to_all | solution.py:156
  322.3 0.8 copy.72
  323.1 2.9 collective-permute-start.2
  326.3 8.4 %collective-permute-done.2 = bf16[128,1024]{0,1:T(8,128)(2,1)S(1)} collective-permute-done((bf16[128,1024]{0,1:T(8,128)(2,1)}, bf16[128,1024]{0,1:T(8,128)(2,1)S(1)}, u32[]{:S(2)}, u32[]{:S(2)}) %collective-permute-start.2) | collective-permute-done | bytes 262176 | tf_op jit(solution)/shard_map/ppermute | solution.py:20
  334.7 0.2 fusion.43
  335.1 5.6 %all_to_all.258 = bf16[128,2,512]{2,0,1:T(8,128)(2,1)} all-to-all(bf16[128,2,512]{2,0,1:T(8,128)(2,1)S(1)} %copy.73), channel_id=1, replica_groups=mesh['section'=16,'tensor'=8,'dp'=2] {'dp'}, dimensions={1} | all-to-all | bytes 524288 | tf_op jit(solution)/shard_map/all_to_all | solution.py:125
  340.7 17.5 %reduce-scatter.9.cloned.1.call-done = f32[256,512]{1,0:T(8,128)} async-done(((f32[256,8192]{1,0:T(8,128)}), f32[256,512]{1,0:T(8,128)}) %reduce-scatter.9.cloned.1.call-update) | async-done | bytes 524304 | tf_op jit(solution)/shard_map/reduce_scatter | solution.py:106
  358.2 1.3 fusion.27
  359.5 7.9 %all_to_all.259 = bf16[2,128,512]{2,1,0:T(8,128)(2,1)S(1)} all-to-all(bf16[2,128,512]{2,1,0:T(8,128)(2,1)S(1)} %bitcast.212), channel_id=1, replica_groups=mesh['section'=16,'tensor'=8,'dp'=2] {'dp'}, dimensions={0} | all-to-all | bytes 524288 | tf_op jit(solution)/shard_map/all_to_all | solution.py:115
  367.6 1.3 collective-permute-start.1
  368.9 1.1 copy.61
  370.0 11.7 %collective-permute-done.1 = bf16[128,1024]{0,1:T(8,128)(2,1)S(1)} collective-permute-done((bf16[128,1024]{0,1:T(8,128)(2,1)S(1)}, bf16[128,1024]{0,1:T(8,128)(2,1)S(1)}, u32[]{:S(2)}, u32[]{:S(2)}) %collective-permute-start.1) | collective-permute-done | bytes 262176 | tf_op jit(solution)/shard_map/ppermute | solution.py:20
  381.9 6.4 %all_to_all.260 = bf16[128,2,512]{2,0,1:T(8,128)(2,1)S(1)} all-to-all(bf16[128,2,512]{2,0,1:T(8,128)(2,1)S(1)} %copy.64), channel_id=1, replica_groups=mesh['section'=16,'tensor'=8,'dp'=2] {'dp'}, dimensions={1} | all-to-all | bytes 524288 | tf_op jit(solution)/shard_map/all_to_all | solution.py:92
  388.3 9.1 %fusion.4 = f32[256,8192]{1,0:T(8,128)} fusion(bf16[256,512]{1,0:T(8,128)(2,1)S(1)} %bitcast.184, bf16[1,512,8192]{2,1,0:T(8,128)(2,1)} %param.15), kind=kOutput, calls=%fused_computation.4 | convolution fusion | flops 2147483648 | bytes 17039360 | tf_op jit(solution)/shard_map/dot_general | solution.py:107
  397.4 4.0 all_to_all.261
  401.6 3.9 all_to_all.262
  405.9 0.3 copy.60
  406.2 0.9 broadcast_in_dim.10
  407.1 0.3 fusion.100
  407.4 0.3 fusion.75
  407.8 55.9 %all-reduce.10 = (bf16[256,128]{1,0:T(8,128)(2,1)S(1)}, bf16[256,128]{1,0:T(8,128)(2,1)S(1)}, bf16[256,128]{1,0:T(8,128)(2,1)S(1)}, bf16[256,128]{1,0:T(8,128)(2,1)S(1)}) all-reduce(f32[256,128]{1,0:T(8,128)S(1)} %fusion.75, f32[256,128]{1,0:T(8,128)S(1)} %fusion.47, ...), channel_id=1, replica_groups=mesh['section'=16,'tensor'=8,'dp'=2] {'tensor','dp'}, use_global_device_ids=true, to_apply=%region_7.0 | all-reduce | flops 131072 | bytes 786432 | tf_op jit(solution)/shard_map/psum | solution.py:93
  464.0 0.9 fusion.31
  464.9 1.0 fusion.33
  465.9 7.2 %fusion.21 = f32[256,512]{1,0:T(8,128)S(1)} fusion(bf16[256,8192]{1,0:T(8,128)(2,1)} %all-gather.5.cloned.1.call-done, bf16[1,512,8192]{2,1,0:T(8,128)(2,1)} %param.15, bf16[256,512]{1,0:T(8,128)(2,1)S(1)} %bitcast.196), kind=kOutput, calls=%fused_computation.25 | convolution fusion | flops 2147745792 | bytes 13369344 | tf_op jit(solution)/shard_map/dot_general | solution.py:136
  473.3 8.3 %all_to_all.263 = bf16[2,128,512]{2,1,0:T(8,128)(2,1)S(1)} all-to-all(bf16[2,128,512]{2,1,0:T(8,128)(2,1)S(1)} %bitcast.215), channel_id=1, replica_groups=mesh['section'=16,'tensor'=8,'dp'=2] {'dp'}, dimensions={0} | all-to-all | bytes 524288 | tf_op jit(solution)/shard_map/all_to_all | solution.py:156
  481.7 0.3 copy.74
  482.0 0.9 broadcast_in_dim.12
  482.9 1.3 fusion.26
  484.2 7.3 %all_to_all.264 = bf16[2,128,512]{2,1,0:T(8,128)(2,1)S(1)} all-to-all(bf16[2,128,512]{2,1,0:T(8,128)(2,1)S(1)} %bitcast.214), channel_id=1, replica_groups=mesh['section'=16,'tensor'=8,'dp'=2] {'dp'}, dimensions={0} | all-to-all | bytes 524288 | tf_op jit(solution)/shard_map/all_to_all | solution.py:115
  491.5 0.3 copy.65
  491.7 0.9 broadcast_in_dim.11
  (63 shorter events, 4.7 us)
Async XLA Ops:
  7.2 89.5 %reduce-scatter.5.cloned.1.call-start = ((), (), s32[]{:S(2)}) async-start(), calls=%async_computation.18 | async-start | bytes 8912896 | tf_op jit(solution)/shard_map/reduce_scatter | solution.py:100
  22.9 0.9 copy-start
  22.9 73.7 %copy-start.1 = (bf16[1,128,512]{2,1,0:T(8,128)(2,1)S(1)}, bf16[1,128,512]{2,1,0:T(8,128)(2,1)}, u32[]{:S(2)}) copy-start(bf16[1,128,512]{2,1,0:T(8,128)(2,1)} %param.17) | copy-start | bytes 393220
  22.9 84.7 %copy-start.7 = (bf16[1,128,1024]{2,1,0:T(8,128)(2,1)S(1)}, bf16[1,128,1024]{2,1,0:T(8,128)(2,1)}, u32[]{:S(2)}) copy-start(bf16[1,128,1024]{2,1,0:T(8,128)(2,1)} %param.24) | copy-start | bytes 786436
  22.9 181.1 %reduce-scatter.7.cloned.1.call-start = ((), (), s32[]{:S(2)}) async-start(), calls=%async_computation.19 | async-start | bytes 8912896 | tf_op jit(solution)/shard_map/reduce_scatter | solution.py:100
  106.1 10.9 %collective-permute-start = (bf16[128,1024]{0,1:T(8,128)(2,1)S(1)}, bf16[128,1024]{0,1:T(8,128)(2,1)S(1)}, u32[]{:S(2)}, u32[]{:S(2)}) collective-permute-start(bf16[128,1024]{0,1:T(8,128)(2,1)S(1)} %bitcast.217), channel_id=1, source_target_pairs={{0,16},{16,32},{32,48},{48,64},{64,80},{80,96},{96,112},{112,128},... | collective-permute-start | bytes 786440 | tf_op jit(solution)/shard_map/ppermute | solution.py:20
  131.0 1.0 copy-start.5
  131.0 1.9 copy-start.8
  131.0 3.1 copy-start.10
  131.0 95.3 %copy-start.9 = (s32[2,128]{1,0:T(2,128)S(1)}, s32[2,128]{1,0:T(2,128)}, u32[]{:S(2)}) copy-start(s32[2,128]{1,0:T(2,128)} %param.28) | copy-start | bytes 3076
  131.0 176.3 %all-gather.3.cloned.1.call-start = ((), (), s32[]{:S(2)}) async-start(), calls=%async_computation.22 | async-start | bytes 4456448 | tf_op jit(solution)/shard_map/all_gather | solution.py:137
  238.5 119.7 %reduce-scatter.9.cloned.1.call-start = ((), (), s32[]{:S(2)}) async-start(), calls=%async_computation.20 | async-start | bytes 8912896 | tf_op jit(solution)/shard_map/reduce_scatter | solution.py:106
  252.7 0.9 copy-start.4
  252.7 1.1 copy-start.2
  252.7 213.2 %all-gather.5.cloned.1.call-start = ((), (), s32[]{:S(2)}) async-start(), calls=%async_computation.23 | async-start | bytes 4456448 | tf_op jit(solution)/shard_map/all_gather | solution.py:137
  307.3 50.9 %copy-start.6 = (bf16[1,128,512]{2,1,0:T(8,128)(2,1)S(1)}, bf16[1,128,512]{2,1,0:T(8,128)(2,1)}, u32[]{:S(2)}) copy-start(bf16[1,128,512]{2,1,0:T(8,128)(2,1)} %param.19) | copy-start | bytes 393220
  323.1 11.6 %collective-permute-start.2 = (bf16[128,1024]{0,1:T(8,128)(2,1)}, bf16[128,1024]{0,1:T(8,128)(2,1)S(1)}, u32[]{:S(2)}, u32[]{:S(2)}) collective-permute-start(bf16[128,1024]{0,1:T(8,128)(2,1)} %bitcast.44), channel_id=1, source_target_pairs={{16,0},{32,16},{48,32},{64,48},{80,64},{96,80},{112,96},{128,112},... | collective-permute-start | bytes 786440 | tf_op jit(solution)/shard_map/ppermute | solution.py:20
  340.7 142.2 %reduce-scatter.11.cloned.1.call-start = ((), (), s32[]{:S(2)}) async-start(), calls=%async_computation.21 | async-start | bytes 8912896 | tf_op jit(solution)/shard_map/reduce_scatter | solution.py:106
  367.6 14.1 %collective-permute-start.1 = (bf16[128,1024]{0,1:T(8,128)(2,1)S(1)}, bf16[128,1024]{0,1:T(8,128)(2,1)S(1)}, u32[]{:S(2)}, u32[]{:S(2)}) collective-permute-start(bf16[128,1024]{0,1:T(8,128)(2,1)S(1)} %bitcast.218), channel_id=1, source_target_pairs={{0,16},{16,32},{32,48},{48,64},{64,80},{80,96},{96,112},{112,128},... | collective-permute-start | bytes 786440 | tf_op jit(solution)/shard_map/ppermute | solution.py:20
  397.3 10.3 %copy-start.3 = (bf16[128,2,512]{2,0,1:T(8,128)(2,1)S(1)}, bf16[128,2,512]{2,0,1:T(8,128)(2,1)}, u32[]{:S(2)}) copy-start(bf16[128,2,512]{2,0,1:T(8,128)(2,1)} %all_to_all.258) | copy-start | bytes 786436
Sparse Core Ops, SparseCore 0:
  23.1 73.5 reduce-scatter.4
  131.1 72.8 reduce-scatter.6
  238.6 39.1 all-gather.2
  280.2 77.9 reduce-scatter.8
  359.9 42.9 all-gather.4
  405.2 77.6 reduce-scatter.10
where the time goes:
time: 504 us; the launch traced here: 499 us
  blocking collectives  315 us (62%)
  waiting for transfers between devices  84.5 us (17%)
  matrix products  60.1 us (12%)
  between operations  17.3 us (3%)
  local copies, waits for them, and re-layouts  15.6 us (3%)
  starting transfers between devices  5.73 us (1%)
    psum x4, blocking collectives, on_device(): lax.psum((jnp.dot(pol_rows, policy_down, preferred_element_type=jnp.float...  213 us
    reduce_scatter x2, waiting for transfers between devices, on_device(): lax.psum_scatter(jnp.dot(pol_rows, weight, preferred_element_type=jnp.flo...  37.5 us
    ppermute x3, waiting for transfers between devices, passed_along(): return lax.ppermute(block, axis, route)  29.3 us
    dot_general x2, matrix products, on_device(): jnp.dot(ref_rows, weight, preferred_element_type=jnp.float32)  18 us
    dot_general x2, matrix products, on_device(): jnp.dot(pol_rows, weight, preferred_element_type=jnp.float32)  17.9 us
    reduce_scatter x2, waiting for transfers between devices, on_device(): lax.psum_scatter(jnp.dot(ref_rows, weight, preferred_element_type=jnp.flo...  17.5 us
    all_to_all x2, blocking collectives, on_device(): lax.all_to_all(result, 'dp', split_axis=0, concat_axis=1, tiled=True)  15.8 us
    all_to_all x2, blocking collectives, on_device(): lax.all_to_all(out_pol, 'dp', split_axis=0, concat_axis=1, tiled=True)  15.3 us
  transfers between devices with their start and end apart: 9, of which 7 were waited for; matrix products, arithmetic and copies ran while one was open for 9% of the time, Pallas kernels for 0%

commit v1 on v0

v1 whole, which is shorter than its diff:
```python
import functools

import jax
import jax.numpy as jnp
from jax import lax
from jax.experimental import pallas as pl
from jax.experimental.pallas import tpu as pltpu
from jax.sharding import PartitionSpec as P

BF = jnp.bfloat16
F32 = jnp.float32
MESH = pl.DeviceIdType.MESH

NX, NY = 2, 4
NT = NX * NY
ROUTE_ROWS = 128

ADAPTER_SCALE = 0.5
MIX_WEIGHT = 0.6
PREF_BETA = 0.1
LOSS_SCALE = 1024.0
NORM_EPSILON = 1e-06


def nn(a, b):
    return lax.dot_general(a, b, (((1,), (0,)), ((), ())), preferred_element_type=F32)


def nt(a, b):
    return lax.dot_general(a, b, (((1,), (1,)), ((), ())), preferred_element_type=F32)


def tn(a, b):
    return lax.dot_general(a, b, (((0,), (0,)), ((), ())), preferred_element_type=F32)


def mixed(first, second):
    return (MIX_WEIGHT * first.astype(F32) + (1.0 - MIX_WEIGHT) * second.astype(F32)).astype(BF)


def scratch(tok, cb, rank):
    rows, wide = 2 * tok, 2 * cb
    na = ROUTE_ROWS
    nb = rows - na
    ha, hb = na // 2, nb // 2
    piece = tok // NT
    vm = lambda *shape: pltpu.VMEM(shape, BF)
    vf = lambda *shape: pltpu.VMEM(shape, F32)
    dma = lambda *shape: pltpu.SemaphoreType.DMA(shape)
    table = {
        "wb": vm(NX, NY, wide, cb),
        "xin": vm(4, rows, wide),
        "st": vm(2, tok, wide),
        "sb": vm(2, rows, cb),
        "tg": vm(2, rows, cb),
        "dn": vm(wide, rank),
        "do": vm(wide, rank),
        "dr": vm(wide, rank),
        "ur": vm(rank, cb),
        "ax": vf(2, 8, tok),
        "pb": vm(4, NX, NY, rows, cb),
        "ra1": vm(4, 4, na, cb),
        "ra2": vm(4, 2, ha, cb),
        "ra3": vm(4, 2, na, cb),
        "rb1": vm(4, 2, NX, hb, cb),
        "rb2": vm(4, 2, NX, nb, cb),
        "rb3": vm(4, nb, cb),
        "po": vm(4, rows, cb),
        "gb": vm(2, NX, NY, rows, cb),
        "acc": vf(2, rows, cb),
        "bs": vm(2, rows, cb),
        "br": vm(2, rows, cb),
        "co": vm(2, rows, cb),
        "bps": vm(2, rows, rank),
        "bpr": vm(2, tok, rank),
        "hi": vf(2, 2 * NT, 8, rows),
    }
    for i, parts in enumerate((4, 1, 2, 1)):
        table[f"ls{i}"] = vm(tok, parts * rank)
        table[f"ai{i}"] = vm(NT, piece, parts * rank)
        table[f"ao{i}"] = vm(rows, parts * rank)
    table.update(
        {
            "l_sem": dma(24),
            "e_send": dma(24),
            "e_recv": dma(24),
            "r_send": dma(4, 13),
            "r_recv": dma(4, 13),
            "g_send": dma(2, 13),
            "g_recv": dma(2, 13),
            "a_send": dma(4, 3),
            "a_recv": dma(4, 3),
            "h_send": dma(2),
            "h_recv": dma(2),
            "p_send": dma(3),
            "p_recv": dma(3),
            "m_send": dma(9),
            "m_recv": dma(9),
        }
    )
    return table


def kernel(
    names,
    sections,
    width,
    base_weight,
    pol_down,
    pol_up,
    old_down,
    old_up,
    pol_in,
    ref_in,
    grad_in,
    stash,
    fresh_pol,
    fresh_ref,
    targets,
    final_gain,
    token_side,
    ref_logratio,
    pol_out,
    ref_out,
    grad_out,
    grad_down,
    grad_up,
    *buffers,
):
    b = dict(zip(names, buffers))
    wb, xin, pb, gb = b["wb"], b["xin"], b["pb"], b["gb"]
    rows, wide = xin.shape[1:]
    tok, cb = rows // 2, wide // 2
    rank = pol_up.shape[1]
    na = ROUTE_ROWS
    nb = rows - na
    ha, hb = na // 2, nb // 2
    piece = tok // NT

    s = lax.axis_index("section")
    t = lax.axis_index("tensor")
    c = lax.axis_index("dp")
    x, y = t // NY, t % NY
    ox, oc = 1 - x, 1 - c
    y1, y2, y3 = (y + 1) % NY, (y + 2) % NY, (y + 3) % NY
    is_last = s == sections - 1
    is_first = s == 0
    pair = (s, t, oc)
    over = (s, ox * NY + y, c)
    plus = (s, x * NY + y1, c)
    minus = (s, x * NY + y3, c)

    my_rows = pl.ds(pl.multiple_of(c * tok, tok), tok)
    its_rows = pl.ds(pl.multiple_of(oc * tok, tok), tok)
    my_cols = pl.ds(pl.multiple_of(c * cb, cb), cb)
    its_cols = pl.ds(pl.multiple_of(oc * cb, cb), cb)
    my_deep = my_cols
    a_rows, b_rows = pl.ds(0, na), pl.ds(na, nb)

    def send(src, dst, group, index, device):
        return pltpu.make_async_remote_copy(
            src_ref=src,
            dst_ref=dst,
            send_sem=b[group + "_send"].at[index],
            recv_sem=b[group + "_recv"].at[index],
            device_id=device,
            device_id_type=MESH,
        )

    finals = []

    def start(copy):
        copy.start()
        finals.append(copy)

    def weight_cols(xx, yy, core):
        first = pl.multiple_of((xx * NY + yy) * wide + core * cb, cb)
        return base_weight.at[0, :, pl.ds(first, cb)]

    def chunk_of(j):
        step = jnp.where(j == 0, 2, jnp.where(j == 3, 0, 2 * j - 1))
        return (y + step) % NY

    def weight_local(j, side):
        xx, yy = (ox if side == 0 else x), chunk_of(j)
        return pltpu.make_async_copy(
            weight_cols(xx, yy, c), wb.at[xx, yy, my_deep, :], b["l_sem"].at[2 * j + side]
        )

    def weight_remote(j, side):
        xx, yy = (ox if side == 0 else x), chunk_of(j)
        return send(weight_cols(xx, yy, oc), wb.at[xx, yy, my_deep, :], "e", 2 * j + side, pair)

    own = {
        "dn": (pol_down.at[0], b["dn"].at[my_deep]),
        "do": (old_down.at[0], b["do"].at[my_deep]),
        "p0": (pol_in.at[0], xin.at[0, my_rows]),
        "r0": (ref_in.at[0], xin.at[1, my_rows]),
        "g0": (grad_in.at[0, :, my_cols], gb.at[0, x, y, my_rows]),
        "s0": (stash.at[0, 0, :, my_cols], b["sb"].at[0, my_rows]),
        "s1": (stash.at[0, 1, :, my_cols], b["sb"].at[1, my_rows]),
        "t0": (targets.at[0, :, my_cols], b["tg"].at[0, my_rows]),
        "t1": (targets.at[1, :, my_cols], b["tg"].at[1, my_rows]),
        "st": (stash.at[0], b["st"]),
        "fp": (fresh_pol.at[0], xin.at[2, my_rows]),
        "fr": (fresh_ref.at[0], xin.at[3, my_rows]),
    }
    away = {
        "dn": (pol_down.at[0], b["dn"].at[my_deep]),
        "do": (old_down.at[0], b["do"].at[my_deep]),
        "p0": (pol_in.at[0], xin.at[0, my_rows]),
        "r0": (ref_in.at[0], xin.at[1, my_rows]),
        "g0": (grad_in.at[0, :, its_cols], gb.at[0, x, y, my_rows]),
        "s0": (stash.at[0, 0, :, its_cols], b["sb"].at[0, my_rows]),
        "s1": (stash.at[0, 1, :, its_cols], b["sb"].at[1, my_rows]),
        "t0": (targets.at[0, :, its_cols], b["tg"].at[0, my_rows]),
        "t1": (targets.at[1, :, its_cols], b["tg"].at[1, my_rows]),
        "ax": (b["ax"].at[c], b["ax"].at[c]),
        "fp": (fresh_pol.at[0], xin.at[2, my_rows]),
        "fr": (fresh_ref.at[0], xin.at[3, my_rows]),
    }
    place = {name: 8 + i for i, name in enumerate(["dn", "do", "p0", "r0", "g0", "s0", "s1", "t0", "t1", "st", "fp", "fr", "ax"])}

    def local(name):
        return pltpu.make_async_copy(*own[name], b["l_sem"].at[place[name]])

    def swap(name):
        return send(*away[name], "e", place[name], pair)

    for name in ("dn", "do", "p0", "r0", "st"):
        local(name).start()
    for j in range(4):
        for side in range(2):
            weight_local(j, side).start()
    for name in ("g0", "s0", "s1", "t0", "t1"):
        local(name).start()

    @pl.when(is_first)
    def _():
        local("fp").start()
        local("fr").start()

    me = 2 * t + c
    barrier = pltpu.get_barrier_semaphore()

    def greet(d, _):
        other = (me + d) % (2 * NT)
        pl.semaphore_signal(barrier, inc=1, device_id=(s, other // 2, other % 2), device_id_type=MESH)
        return 0

    after = ((s + 1) % sections, t, c)
    before = ((s + sections - 1) % sections, t, c)
    lax.fori_loop(1, 2 * NT, greet, 0)
    pl.semaphore_signal(barrier, inc=1, device_id=after, device_id_type=MESH)
    pl.semaphore_signal(barrier, inc=1, device_id=before, device_id_type=MESH)
    pl.semaphore_wait(barrier, 2 * NT + 1)

    start(swap("dn"))
    start(swap("do"))
    start(swap("p0"))
    for j in range(4):
        for side in range(2):
            start(weight_remote(j, side))
    start(swap("r0"))

    side = token_side[...]
    signs = (side == 1).astype(F32) - (side == 2).astype(F32)
    ratios = jnp.broadcast_to(ref_logratio[...], (2, tok))
    b["ax"][c] = jnp.concatenate([signs, ratios, signs, ratios], axis=0)
    for name in ("ax", "t0", "g0", "s0", "s1", "t1"):
        start(swap(name))

    @pl.when(is_first)
    def _():
        swap("fp").start()
        swap("fr").start()

    def part_rows(index):
        return pl.ds(pl.multiple_of(index * piece, piece), piece)

    def sum_send(i):
        ls, ai = b[f"ls{i}"], b[f"ai{i}"]

        def one(d, _):
            tt = (t + d) % NT
            send(ls.at[part_rows(tt)], ai.at[t], "a", (i, 0), (s, tt, c)).start()
            return 0

        lax.fori_loop(1, NT, one, 0)
        ai[t] = ls[part_rows(t)]

    def sum_reduce(i):
        ai, ao = b[f"ai{i}"], b[f"ao{i}"]
        seven = ai.at[pl.ds(0, NT - 1)]
        pltpu.make_async_copy(seven, seven, b["a_recv"].at[i, 0]).wait()
        total = ai[0].astype(F32)
        for d in range(1, NT):
            total += ai[d].astype(F32)
        here = pl.ds(pl.multiple_of(c * tok + t * piece, piece), piece)
        ao[here] = total.astype(BF)

        def one(d, _):
            tt = (t + d) % NT
            send(ao.at[here], ao.at[here], "a", (i, 1), (s, tt, c)).start()
            return 0

        lax.fori_loop(1, NT, one, 0)

    def sum_share(i):
        ao = b[f"ao{i}"]
        most = ao.at[pl.ds(0, piece * (NT - 1))]
        pltpu.make_async_copy(most, most, b["a_recv"].at[i, 1]).wait()
        start(send(ao.at[my_rows], ao.at[my_rows], "a", (i, 2), pair))

    def sum_done(i):
        ao = b[f"ao{i}"]
        send(ao.at[my_rows], ao.at[my_rows], "a", (i, 2), pair).wait_recv()

    def sum_sent(i):
        seven = b[f"ai{i}"].at[pl.ds(0, NT - 1)]
        pltpu.make_async_copy(seven, seven, b["a_send"].at[i, 0]).wait()
        most = b[f"ao{i}"].at[pl.ds(0, piece * (NT - 1))]
        pltpu.make_async_copy(most, most, b["a_send"].at[i, 1]).wait()

    def f32(ref, *index):
        return ref[index].astype(F32)

    def a1(p, j):
        return send(pb.at[p, ox, chunk_of(j), a_rows], b["ra1"].at[p, j], "r", (p, j), over)

    def a2(p, up):
        half = pl.ds(0, ha) if up == 0 else pl.ds(ha, ha)
        return send(pb.at[p, x, y2, half], b["ra2"].at[p, up], "r", (p, 4 + up), plus if up == 0 else minus)

    def b1(p, up):
        half = pl.ds(na, hb) if up == 0 else pl.ds(na + hb, hb)
        return send(pb.at[p, :, y2, half], b["rb1"].at[p, up], "r", (p, 6 + up), plus if up == 0 else minus)

    def b2(p, up):
        yy = y1 if up == 0 else y3
        return send(pb.at[p, :, yy, b_rows], b["rb2"].at[p, up], "r", (p, 8 + up), plus if up == 0 else minus)

    def b3(p):
        return send(pb.at[p, ox, y, b_rows], b["rb3"].at[p], "r", (p, 10), over)

    def a3(p, up):
        yy = y1 if up == 0 else y3
        return send(pb.at[p, x, yy, a_rows], b["ra3"].at[p, up], "r", (p, 11 + up), plus if up == 0 else minus)

    def products(p, first):
        def body(j, _):
            yy = chunk_of(j)
            for which in range(2):
                xx = ox if which == 0 else x
                if first:
                    weight_local(j, which).wait()
                    weight_remote(j, which).wait_recv()
                pb[p, xx, yy] = nn(xin[p], wb[xx, yy]).astype(BF)
                if first and which == 0:
                    a1(p, j).start()
            return 0

        lax.fori_loop(0, 4, body, 0)
        if first:
            finals.extend(a1(p, j) for j in range(4))

    def stage1(p, first):
        if not first:
            start(a1(p, 0))
        start(b1(p, 0))
        start(b1(p, 1))
        if not first:
            for j in range(1, 4):
                start(a1(p, j))

    def stage2(p):
        for up in range(2):
            yy = y1 if up == 0 else y3
            half = pl.ds(na, hb) if up == 0 else pl.ds(na + hb, hb)
            b1(p, up).wait_recv()
            for xx in range(NX):
                pb[p, xx, yy, half] = (f32(pb, p, xx, yy, half) + f32(b["rb1"], p, up, xx)).astype(BF)
            start(b2(p, up))

    def stage3(p):
        a1(p, 0).wait_recv()
        pb[p, x, y2, a_rows] = (f32(pb, p, x, y2, a_rows) + f32(b["ra1"], p, 0)).astype(BF)
        start(a2(p, 0))
        start(a2(p, 1))

    def stage4(p):
        b2(p, 0).wait_recv()
        b2(p, 1).wait_recv()
        pb[p, ox, y, b_rows] = (
            f32(pb, p, ox, y, b_rows) + f32(b["rb2"], p, 0, ox) + f32(b["rb2"], p, 1, ox)
        ).astype(BF)
        start(b3(p))

    def stage5(p):
        for up in range(2):
            yy = y1 if up == 0 else y3
            half = pl.ds(0, ha) if up == 0 else pl.ds(ha, ha)
            rest = pl.ds(ha, ha) if up == 0 else pl.ds(0, ha)
            a1(p, 1 + up).wait_recv()
            a2(p, up).wait_recv()
            pb[p, x, yy, half] = (
                f32(pb, p, x, yy, half) + f32(b["ra1"], p, 1 + up, half) + f32(b["ra2"], p, up)
            ).astype(BF)
            pb[p, x, yy, rest] = (f32(pb, p, x, yy, rest) + f32(b["ra1"], p, 1 + up, rest)).astype(BF)
            start(a3(p, up))

    def finish(p, low, up_ref):
        a1(p, 3).wait_recv()
        a3(p, 0).wait_recv()
        a3(p, 1).wait_recv()
        b3(p).wait_recv()
        summed = (
            f32(pb, p, x, y, a_rows)
            + f32(b["ra1"], p, 3)
            + f32(b["ra3"], p, 0)
            + f32(b["ra3"], p, 1),
            f32(pb, p, x, y, b_rows)
            + f32(b["rb2"], p, 0, x)
            + f32(b["rb2"], p, 1, x)
            + f32(b["rb3"], p),
        )
        for part, total in zip((a_rows, b_rows), summed):
            adapted = ADAPTER_SCALE * nn(low[0][part, low[1]], up_ref)
            b["po"][p, part] = (f32(xin, p, part, my_cols) + total + adapted).astype(BF)

    gain = lambda: final_gain[:, my_cols]

    def head_sums(k):
        @pl.when(is_last)
        def _():
            h = f32(b["po"], 2 * k)
            squares = jnp.sum(h * h, axis=1, keepdims=True)
            inner = jnp.sum(h * gain() * f32(b["tg"], k), axis=1, keepdims=True)
            lane = lax.broadcasted_iota(jnp.int32, (rows, 128), 1)
            both = jnp.where(lane == 0, squares, inner).T
            b["hi"][k, me] = both[:8]

            def one(d, _):
                other = (me + d) % (2 * NT)
                slot = b["hi"].at[k, me]
                send(slot, slot, "h", k, (s, other // 2, other % 2)).start()
                return 0

            lax.fori_loop(1, 2 * NT, one, 0)

    def head_cotangent(k):
        @pl.when(is_last)
        def _():
            others = b["hi"].at[k, pl.ds(0, 2 * NT - 1)]
            pltpu.make_async_copy(others, others, b["h_recv"].at[k]).wait()
            total = b["hi"][k, 0]
            for d in range(1, 2 * NT):
                total += b["hi"][k, d]
            sums = jnp.concatenate([total] * 16, axis=0).T
            squares, inner = sums[:, 0:1], sums[:, 1:2]
            rms = lax.rsqrt(squares / width + NORM_EPSILON)
            for p in range(2):
                part = slice(p * tok, (p + 1) * tok)
                aux = jnp.concatenate([b["ax"][p]] * (tok // 8), axis=0).T
                sign, ratio = aux[:, k : k + 1], aux[0:1, 2 + k : 3 + k]
                r, dot = rms[part], inner[part]
                margin = PREF_BETA * (jnp.sum(dot * r * sign, axis=0, keepdims=True) - ratio)
                weight = -LOSS_SCALE * PREF_BETA * jax.nn.sigmoid(-margin) * sign
                h = f32(b["po"], 2 * k, part)
                g = weight * (r * gain() * f32(b["tg"], k, part) - (dot * r * r * r / width) * h)
                gb[k, x, y, part] = g.astype(BF)

            pltpu.make_async_copy(others, others, b["h_send"].at[k]).wait()

    def g_copy(k, i):
        own_x, away_x, full = x, ox, pl.ds(0, rows)
        first, second = pl.ds(0, tok), pl.ds(tok, tok)
        xx, yy, part, device = (
            (own_x, y, full, plus),
            (own_x, y, full, minus),
            (own_x, y, a_rows, over),
            (own_x, y, b_rows, over),
            (away_x, y, a_rows, plus),
            (away_x, y, a_rows, minus),
            (own_x, y3, first, plus),
            (own_x, y1, second, minus),
            (own_x, y3, b_rows, over),
            (own_x, y1, b_rows, over),
            (away_x, y3, pl.ds(0, ha), plus),
            (away_x, y1, pl.ds(ha, ha), minus),
            (own_x, y2, b_rows, over),
        )[i]
        block = gb.at[k, xx, yy, part]
        return send(block, block, "g", (k, i), device)

    def g_start(k, *which):
        for i in which:
            start(g_copy(k, i))

    def g_wait(k, *which):
        for i in which:
            g_copy(k, i).wait_recv()

    def gather1(k):
        g_start(k, 2, 0, 1, 3)

    def gather2(k):
        g_wait(k, 2)
        g_start(k, 4, 5)

    def gather3(k):
        g_wait(k, 0)
        g_start(k, 6, 8)
        g_wait(k, 1)
        g_start(k, 7, 9)

    def gather4(k):
        g_wait(k, 4)
        g_start(k, 10)
        g_wait(k, 5)
        g_start(k, 11)

    def gather5(k):
        g_wait(k, 6, 7)
        g_start(k, 12)

    def through(k, xx, yys, fresh=False):
        def body(j, _):
            yy = (y + j) % NY
            for core in range(2):
                deep = pl.ds(core * cb, cb)
                term = nt(gb[k, xx, yy], wb[xx, yy, deep])
                if fresh:
                    b["acc"][core] = jnp.where(j == yys[0], term, b["acc"][core] + term)
                else:
                    b["acc"][core] += term
            return 0

        lax.fori_loop(yys[0], yys[1], body, 0)

    def products_back(k):
        for core in range(2):
            b["acc"][core] = jnp.zeros((rows, cb), F32)
        through(k, x, (0, NY))
        g_wait(k, 3, 8, 9, 10, 11, 12)
        through(k, ox, (0, NY))
        b["bs"][k] = b["acc"][oc].astype(BF)
        start(send(b["bs"].at[k], b["br"].at[k], "m", k, pair))

    def back_start(k):
        b["bps"][k] = nt(gb[k, x, y], pol_up[0]).astype(BF)
        start(send(b["bps"].at[k, its_rows], b["bpr"].at[k], "m", 2 + k, pair))

    def back_sum(k, i):
        send(b["bps"].at[k, its_rows], b["bpr"].at[k], "m", 2 + k, pair).wait_recv()
        b[f"ls{i}"][...] = (f32(b["bps"], k, my_rows) + f32(b["bpr"], k)).astype(BF)
        sum_send(i)

    def back_finish(k, i):
        send(b["bs"].at[k], b["br"].at[k], "m", k, pair).wait_recv()
        back = b[f"ao{i}"][...]
        adapted = ADAPTER_SCALE * nt(back, b["dn"][my_deep])
        b["co"][k] = (f32(gb, k, x, y) + b["acc"][c] + f32(b["br"], k) + adapted).astype(BF)

    def gradients(k, i):
        back = b[f"ao{i}"][...]
        stored = jnp.where(is_last, xin[2 * k, :, my_cols], b["sb"][k])
        low_pol = b["ao0"][:, 0:rank] if k == 0 else b["ao2"][:, 0:rank]
        low = jnp.where(is_last, low_pol, b["ao0"][:, (2 + k) * rank : (3 + k) * rank])
        down = ADAPTER_SCALE * tn(stored, back)
        up = ADAPTER_SCALE * tn(low, gb[k, x, y])
        if k == 0:
            grad_down[0] = down
            grad_up[0] = up
        else:
            grad_down[0] += down
            grad_up[0] += up

    def pass_copy(i):
        if i < 2:
            return send(b["po"].at[i], xin.at[2 + i, :, my_cols], "p", i, after)
        return send(b["co"].at[0], gb.at[1, x, y], "p", 2, before)

    def pass_on(i):
        @pl.when(is_first if i == 2 else is_last)
        def _():
            pass

        @pl.when(jnp.logical_not(is_first if i == 2 else is_last))
        def _():
            pass_copy(i).start()

    def pass_sent(i):
        @pl.when(jnp.logical_not(is_first if i == 2 else is_last))
        def _():
            pass_copy(i).wait_send()

    def taken(i):
        block = xin.at[2 + i, :, my_cols]
        return send(block, block, "m", 4 + i, pair)

    def take(i):
        @pl.when(jnp.logical_not(is_first))
        def _():
            pass_copy(i).wait_recv()
            taken(i).start()

    def take_done(i):
        name = ("fp", "fr")[i]

        @pl.when(is_first)
        def _():
            local(name).wait()
            swap(name).wait()

        @pl.when(jnp.logical_not(is_first))
        def _():
            taken(i).wait()

    def out_copy(i, src, out):
        return send(src.at[its_rows], out.at[0, :, my_cols], "m", 6 + i, pair)

    def put_out(i, src, out):
        start(out_copy(i, src, out))
        out[0, :, my_cols] = src[my_rows]

    for name in ("dn", "do", "p0", "r0", "st"):
        local(name).wait()
    swap("dn").wait_recv()
    swap("do").wait_recv()
    b["dr"][...] = mixed(b["dn"][...], b["do"][...])
    b["ur"][...] = mixed(pol_up[0], old_up[0])
    for q, (ref, down) in enumerate(
        (
            (xin.at[0, my_rows], b["dn"]),
            (xin.at[1, my_rows], b["dr"]),
            (b["st"].at[0], b["dn"]),
            (b["st"].at[1], b["dn"]),
        )
    ):
        b["ls0"][:, q * rank : (q + 1) * rank] = nn(ref[...], down[...]).astype(BF)
    sum_send(0)
    swap("p0").wait_recv()
    products(0, True)
    stage1(0, True)
    sum_reduce(0)
    stage2(0)
    stage3(0)
    swap("r0").wait_recv()
    products(1, False)
    sum_share(0)
    stage4(0)
    stage1(1, False)
    stage5(0)
    stage2(1)
    sum_done(0)
    finish(0, (b["ao0"], pl.ds(0, rank)), pol_up[0])
    pass_on(0)
    for name in ("g0", "s0", "s1", "t0", "t1"):
        local(name).wait()
        swap(name).wait_recv()
    swap("ax").wait_recv()
    head_sums(0)
    stage3(1)
    stage4(1)
    head_cotangent(0)
    gather1(0)
    back_start(0)
    stage5(1)
    gather2(0)
    back_sum(0, 1)
    finish(1, (b["ao0"], pl.ds(rank, rank)), b["ur"][...])
    pass_on(1)
    gather3(0)
    take(0)
    gather4(0)
    sum_reduce(1)
    take_done(0)
    products(2, False)
    gather5(0)
    stage1(2, False)
    sum_share(1)
    products_back(0)
    take(1)
    stage2(2)
    stage3(2)
    sum_done(1)
    back_finish(0, 1)
    pass_on(2)
    gradients_early = functools.partial(gradients, 0, 1)
    take_done(1)
    for q, down in enumerate((b["dn"], b["dr"])):
        b["ls2"][:, q * rank : (q + 1) * rank] = nn(xin[2 + q, my_rows], down[...]).astype(BF)
    sum_send(2)
    products(3, False)
    stage4(2)
    stage1(3, False)
    sum_reduce(2)
    gradients_early()
    stage5(2)
    stage2(3)
    sum_share(2)
    sum_done(2)
    finish(2, (b["ao2"], pl.ds(0, rank)), pol_up[0])
    head_sums(1)
    put_out(0, b["po"].at[2], pol_out)
    stage3(3)
    stage4(3)
    head_cotangent(1)

    @pl.when(jnp.logical_not(is_last))
    def _():
        pass_copy(2).wait_recv()

    gather1(1)
    back_start(1)
    stage5(3)
    gather2(1)
    back_sum(1, 3)
    finish(3, (b["ao2"], pl.ds(rank, rank)), b["ur"][...])
    put_out(1, b["po"].at[3], ref_out)
    gather3(1)
    gather4(1)
    sum_reduce(3)
    gather5(1)
    sum_share(3)
    sum_done(3)
    gradients(1, 3)
    products_back(1)
    back_finish(1, 3)
    put_out(2, b["co"].at[1], grad_out)

    out_copy(0, b["po"].at[2], pol_out).wait_recv()
    out_copy(1, b["po"].at[3], ref_out).wait_recv()
    out_copy(2, b["co"].at[1], grad_out).wait_recv()
    for copy in finals:
        copy.wait_send()
    for i in range(3):
        pass_sent(i)
    for i in range(4):
        sum_sent(i)


def on_device(sections, width, *operands):
    pol_in = operands[5]
    tok, wide = pol_in.shape[1:]
    cb = wide // 2
    rank = operands[1].shape[2]
    operands = list(operands)
    operands[12] = operands[12].reshape(1, wide)
    table = scratch(tok, cb, rank)
    anywhere = pl.BlockSpec(memory_space=pl.ANY)
    inside = pl.BlockSpec(memory_space=pltpu.VMEM)
    in_vmem = (2, 4, 12, 13, 14)
    outs = (
        jax.ShapeDtypeStruct((1, tok, wide), BF),
        jax.ShapeDtypeStruct((1, tok, wide), BF),
        jax.ShapeDtypeStruct((1, tok, wide), BF),
        jax.ShapeDtypeStruct((1, cb, rank), F32),
        jax.ShapeDtypeStruct((1, rank, cb), F32),
    )
    return pl.pallas_call(
        functools.partial(kernel, tuple(table), sections, width),
        out_shape=outs,
        in_specs=[inside if i in in_vmem else anywhere for i in range(15)],
        out_specs=[inside] * 5,
        scratch_shapes=list(table.values()),
        compiler_params=pltpu.CompilerParams(
            collective_id=0, has_side_effects=True, vmem_limit_bytes=56 * 1024 * 1024
        ),
        name="relay",
    )(*operands)


def solution(mesh):
    in_specs = (
        P("section", ("tensor", "dp"), None),
        P("section", ("tensor", "dp"), None),
        P("section", None, ("tensor", "dp")),
        P("section", ("tensor", "dp"), None),
        P("section", None, ("tensor", "dp")),
        P("section", "dp", "tensor"),
        P("section", "dp", "tensor"),
        P("section", "dp", "tensor"),
        P("section", None, "dp", "tensor"),
        P(None, "dp", "tensor"),
        P(None, "dp", "tensor"),
        P(None, "dp", "tensor"),
        P("tensor"),
        P(None, "dp"),
        P(None, "dp"),
    )
    out_specs = (
        P("section", "dp", "tensor"),
        P("section", "dp", "tensor"),
        P("section", "dp", "tensor"),
        P("section", ("tensor", "dp"), None),
        P("section", None, ("tensor", "dp")),
    )
    sections = mesh.shape["section"]

    def whole(base_weight, *rest):
        body = functools.partial(on_device, sections, base_weight.shape[1])
        return jax.shard_map(
            body, mesh=mesh, in_specs=in_specs, out_specs=out_specs, check_vma=False
        )(base_weight, *rest)

    return whole
```

time: 504 us -> 158 us (0.31)
  blocking collectives: 315 us -> 0 us
  Pallas kernels: 0 us -> 147 us
  waiting for transfers between devices: 84.5 us -> 0 us
  matrix products: 60.1 us -> 0 us
  between operations: 17.3 us -> 0.64 us
  local copies, waits for them, and re-layouts: 15.6 us -> 9.64 us
  starting transfers between devices: 5.73 us -> 0 us
    psum x5 -> x0, blocking collectives: 227 us -> none  [the longest x4 213 us: on_device(): lax.psum((jnp.dot(pol_rows, policy_down, preferred_element_type=jnp.float...]
    pallas_call x0 -> x1, Pallas kernels: none -> 147 us  [on_device(): pl.pallas_call(functools.partial(kernel, tuple(table), sections, width),...]
    all_to_all x14 -> x0, blocking collectives: 87.6 us -> none  [the longest x2 15.8 us: on_device(): lax.all_to_all(result, 'dp', split_axis=0, concat_axis=1, tiled=True)]
    dot_general x24 -> x0, matrix products: 60.1 us -> none  [the longest x2 18 us: on_device(): jnp.dot(ref_rows, weight, preferred_element_type=jnp.float32)]
    reduce_scatter x4 -> x0, waiting for transfers between devices: 55 us -> none  [the longest x2 37.5 us: on_device(): lax.psum_scatter(jnp.dot(pol_rows, weight, preferred_element_type=jnp.flo...]
    ppermute x3 -> x0, waiting for transfers between devices: 29.3 us -> none  [passed_along(): return lax.ppermute(block, axis, route)]
    ppermute x3 -> x0, starting transfers between devices: 5.48 us -> none  [passed_along(): return lax.ppermute(block, axis, route)]
    unnamed x26 -> x6, local copies, waits for them, and re-layouts: 4.27 us -> 9.64 us
  transfers between devices with their start and end apart: 9 -> 0, of which waited for: 7 -> 0; matrix products, arithmetic and copies ran while one was open for 9% -> 0% of each run, Pallas kernels for 0% -> 0%
where the time goes in v1:
time: 158 us
  Pallas kernels  147 us (93%)
  local copies, waits for them, and re-layouts  9.64 us (6%)
    pallas_call x1, Pallas kernels, on_device(): pl.pallas_call(functools.partial(kernel, tuple(table), sections, width),...  147 us
    unnamed x6, local copies, waits for them, and re-layouts  9.64 us

profile of v1, /device:TPU:229, one launch (start us, length us, event | category | flops | bytes accessed | tf_op | source)
XLA Modules:
  0.0 157.5 jit_solution(2248656540885255374)
XLA Ops:
  0.6 1.3 copy.20.ref_logratio
  1.9 147.2 %relay.1 = (bf16[1,128,1024]{2,1,0:T(8,128)(2,1)}, bf16[1,128,1024]{2,1,0:T(8,128)(2,1)}, bf16[1,128,1024]{2,1,0:T(8,128)(2,1)}, f32[1,512,128]{2,1,0:T(8,128)}, f32[1,128,512]{2,1,0:T(8,128)}) custom-call(bf16[1,512,8192]{2,1,0:T(8,128)(2,1)} %base_weight.1, bf16[1,512,128]{2,1,0:T(8,128)(2,1)} %pol_down.1, bf16[1,128,512]{2,1,0:T(8,128)(2,1)} %pol_up.1, ...), custom_call_target="tpu_custom_call" | custom-call | tf_op jit(solution)/shard_map/relay/pallas_call | solution.py:762
  149.2 1.7 %copy.26 = bf16[1,128,1024]{2,1,0:T(8,128)(2,1)} copy(bf16[1,128,1024]{2,1,0:T(8,128)(2,1)} %get-tuple-element.10) | data formatting | bytes 524288
  150.9 1.7 %copy.27 = bf16[1,128,1024]{2,1,0:T(8,128)(2,1)} copy(bf16[1,128,1024]{2,1,0:T(8,128)(2,1)} %get-tuple-element.11) | data formatting | bytes 524288
  152.5 1.7 %copy.28 = bf16[1,128,1024]{2,1,0:T(8,128)(2,1)} copy(bf16[1,128,1024]{2,1,0:T(8,128)(2,1)} %get-tuple-element.12) | data formatting | bytes 524288
  154.2 1.7 %copy.29 = f32[1,512,128]{2,1,0:T(8,128)} copy(f32[1,512,128]{2,1,0:T(8,128)} %get-tuple-element.13) | data formatting | bytes 524288
  155.9 1.7 %copy.30 = f32[1,128,512]{2,1,0:T(8,128)} copy(f32[1,128,512]{2,1,0:T(8,128)} %get-tuple-element.14) | data formatting | bytes 524288

commit v2 on v0

v2 whole, which is shorter than its diff:
```python
import functools
from types import SimpleNamespace

import jax
import jax.numpy as jnp
from jax import lax
from jax.experimental import pallas as pl
from jax.experimental.pallas import tpu as pltpu
from jax.sharding import PartitionSpec as P

BF = jnp.bfloat16
F32 = jnp.float32
MESH = pl.DeviceIdType.MESH

NX, NY = 2, 4
NT = NX * NY
HALVES = 2
ROWS_LAST = (((48, 80), (64, 48), (32, 80), (48, 48)), ((96, 96), (64, 112)))
ROWS_OTHERS = (((32, 64), (48, 32), (64, 32), (48, 48)), ((112, 80), (80, 96)))

ADAPTER_SCALE = 0.5
MIX_WEIGHT = 0.6
PREF_BETA = 0.1
LOSS_SCALE = 1024.0
NORM_EPSILON = 1e-06

PR, A1, A2, A3, B1, B2, B3, FIN, ARS, ARR, ARH, ARD,     HS, HW, G, TH, BP, ACC, CFIN, CW, TK, TD, GR, END = range(24)
PLAN_LAST = (
    (PR, 0, 0, 0), (B1, 0, 0), (A1, 0, 0, 0), (B1, 0, 1), (A1, 0, 1, 0), (ARS, 0), (PR, 0, 0, 1), (A1, 0, 0, 1),
    (A2, 0, 0), (A1, 0, 1, 1), (B2, 0, 0, 0), (PR, 0, 0, 2), (B2, 0, 0, 1), (A2, 0, 1), (A1, 0, 1, 2), (PR, 1, 0, 0),
    (B1, 1, 0), (B2, 0, 1, 1), (A1, 0, 0, 2), (PR, 0, 0, 3), (A1, 1, 1, 0), (ARR, 0), (B2, 0, 1, 0), (B1, 1, 1),
    (A1, 0, 1, 3), (A3, 0, 1, 1), (B3, 0, 0), (PR, 1, 0, 1), (PR, 1, 0, 2), (A3, 0, 1, 0), (A1, 0, 0, 3),
    (PR, 1, 0, 3), (B3, 0, 1), (A1, 1, 1, 1), (A3, 0, 0, 0), (A3, 0, 0, 1), (B2, 1, 0, 1), (A1, 1, 0, 0), (ARH, 0),
    (B2, 1, 1, 0), (ARD, 0), (A1, 1, 1, 2), (FIN, 0, 1), (HS, 0, 1), (A2, 1, 1), (FIN, 0, 0), (HS, 0, 0),
    (B2, 1, 1, 1), (A1, 1, 0, 2), (A1, 1, 0, 1), (B2, 1, 0, 0), (A2, 1, 0), (A1, 1, 1, 3), (HW, 0, 1), (A1, 1, 0, 3),
    (G, 0, 1, 0), (G, 0, 1, 2), (G, 0, 1, 1), (HW, 0, 0), (G, 0, 0, 2), (BP, 0), (G, 0, 0, 0), (TH, 0, 0),
    (G, 0, 0, 1), (G, 0, 1, 3), (ARS, 1), (B3, 1, 1), (G, 0, 1, 6), (A3, 1, 0, 1), (G, 0, 1, 7), (G, 0, 0, 3),
    (G, 0, 1, 8), (A3, 1, 0, 0), (G, 0, 0, 4), (TK, 0, 0), (G, 0, 0, 8), (G, 0, 0, 9), (G, 0, 0, 7), (TH, 0, 1),
    (A3, 1, 1, 1), (TD, 0, 0), (G, 0, 1, 5), (G, 0, 1, 9), (G, 0, 0, 6), (B3, 1, 0), (G, 0, 0, 5), (ARR, 1),
    (G, 0, 1, 4), (A3, 1, 1, 0), (G, 0, 1, 12), (TK, 0, 1), (TD, 0, 1), (PR, 2, 0, 0), (A1, 2, 1, 0), (G, 0, 0, 12),
    (B1, 2, 0), (PR, 2, 0, 1), (PR, 2, 0, 2), (G, 0, 1, 11), (A1, 2, 0, 0), (A1, 2, 0, 1), (PR, 2, 0, 3), (B1, 2, 1),
    (G, 0, 0, 11), (G, 0, 0, 10), (A1, 2, 0, 2), (TH, 0, 2), (G, 0, 1, 10), (A1, 2, 1, 3), (ARH, 1), (FIN, 1, 1),
    (A1, 2, 1, 1), (B2, 2, 0, 0), (B2, 2, 0, 1), (TH, 0, 3), (A2, 2, 1), (TH, 0, 4), (A1, 2, 1, 2), (FIN, 1, 0),
    (TH, 0, 5), (A1, 2, 0, 3), (TK, 1, 0), (TH, 0, 6), (TH, 0, 7), (TD, 1, 0), (ARD, 1), (ACC, 0, 0), (CFIN, 0),
    (B2, 2, 1, 0), (B2, 2, 1, 1), (TK, 1, 1), (ACC, 0, 1), (TD, 1, 1), (ARS, 2), (CFIN, 1), (A2, 2, 0), (PR, 3, 0, 0),
    (B1, 3, 0), (A3, 2, 1, 0), (PR, 3, 0, 1), (A1, 3, 0, 1), (A3, 2, 1, 1), (ARR, 2), (B1, 3, 1), (B3, 2, 1),
    (A3, 2, 0, 1), (A3, 2, 0, 0), (B3, 2, 0), (B2, 3, 0, 0), (PR, 3, 0, 2), (PR, 3, 0, 3), (A1, 3, 0, 2),
    (B2, 3, 0, 1), (ARH, 2), (ARD, 2), (FIN, 2, 1), (HS, 1, 1), (A1, 3, 1, 1), (FIN, 2, 0), (HS, 1, 0), (B2, 3, 1, 0),
    (A1, 3, 1, 2), (B2, 3, 1, 1), (A1, 3, 0, 0), (B3, 3, 0), (HW, 1, 1), (G, 1, 1, 0), (G, 1, 1, 1), (A1, 3, 1, 0),
    (HW, 1, 0), (G, 1, 0, 0), (G, 1, 0, 1), (G, 1, 1, 2), (G, 1, 0, 2), (G, 1, 0, 3), (BP, 1), (GR, 0), (ARS, 3),
    (G, 1, 1, 3), (B3, 3, 1), (A2, 3, 1), (G, 1, 1, 7), (G, 1, 1, 6), (G, 1, 1, 4), (G, 1, 1, 5), (G, 1, 0, 6),
    (TH, 1, 0), (G, 1, 0, 4), (G, 1, 0, 9), (TH, 1, 1), (G, 1, 0, 8), (TH, 1, 2), (G, 1, 0, 7), (A1, 3, 0, 3),
    (G, 1, 1, 8), (TH, 1, 3), (G, 1, 0, 5), (G, 1, 1, 12), (A2, 3, 0), (ARR, 3), (A3, 3, 1, 0), (G, 1, 1, 9),
    (G, 1, 1, 10), (G, 1, 1, 11), (G, 1, 0, 12), (G, 1, 0, 11), (A1, 3, 1, 3), (G, 1, 0, 10), (TH, 1, 4),
    (A3, 3, 1, 1), (A3, 3, 0, 1), (A3, 3, 0, 0), (ARH, 3), (TH, 1, 5), (TH, 1, 6), (TH, 1, 7), (ACC, 1, 1),
    (ACC, 1, 0), (ARD, 3), (GR, 1), (FIN, 3, 0), (FIN, 3, 1), (END,),
)
PLAN_OTHERS = (
    (G, 0, 0, 0), (G, 0, 0, 2), (G, 0, 0, 1), (G, 0, 1, 3), (PR, 0, 0, 0), (B1, 0, 0), (B1, 0, 1), (PR, 0, 0, 1),
    (A1, 0, 0, 0), (A1, 0, 1, 0), (PR, 1, 0, 0), (ARS, 0), (A1, 1, 1, 0), (PR, 0, 0, 2), (PR, 1, 0, 1), (A1, 1, 0, 0),
    (B1, 1, 0), (G, 0, 0, 3), (G, 0, 0, 8), (A2, 0, 0), (A1, 0, 0, 2), (BP, 0), (A1, 0, 1, 2), (B2, 0, 0, 1),
    (B2, 0, 0, 0), (PR, 1, 0, 2), (A1, 1, 1, 2), (A1, 0, 0, 1), (ARR, 0), (B2, 0, 1, 0), (A2, 0, 1), (B2, 0, 1, 1),
    (B1, 1, 1), (PR, 0, 0, 3), (A1, 0, 1, 1), (A1, 1, 0, 1), (A2, 1, 1), (A1, 0, 0, 3), (PR, 1, 0, 3), (A2, 1, 0),
    (A3, 0, 0, 1), (A3, 0, 0, 0), (G, 0, 1, 0), (TH, 0, 0), (G, 0, 0, 9), (G, 0, 1, 2), (B3, 0, 0), (A1, 1, 1, 1),
    (A1, 1, 0, 3), (A3, 0, 1, 0), (G, 0, 1, 1), (A1, 1, 0, 2), (ARH, 0), (B3, 0, 1), (A3, 0, 1, 1), (ARD, 0),
    (B2, 1, 0, 0), (B2, 1, 0, 1), (A1, 0, 1, 3), (B2, 1, 1, 1), (B2, 1, 1, 0), (FIN, 0, 0), (A3, 1, 0, 1),
    (A3, 1, 1, 0), (TH, 0, 1), (G, 0, 1, 8), (FIN, 0, 1), (A3, 1, 0, 0), (A3, 1, 1, 1), (TH, 0, 2), (TH, 0, 3),
    (B3, 1, 0), (G, 0, 1, 4), (TK, 0, 0), (A1, 1, 1, 3), (G, 0, 0, 7), (G, 0, 1, 9), (G, 0, 1, 6), (G, 0, 0, 5),
    (G, 0, 1, 7), (G, 0, 1, 5), (B3, 1, 1), (ARS, 1), (G, 0, 0, 6), (TK, 0, 1), (FIN, 1, 0), (TD, 0, 0), (TD, 0, 1),
    (G, 0, 0, 4), (PR, 2, 0, 0), (PR, 2, 0, 1), (B1, 2, 1), (PR, 2, 0, 2), (FIN, 1, 1), (B1, 2, 0), (A1, 2, 0, 1),
    (TH, 0, 4), (G, 0, 0, 10), (A1, 2, 1, 0), (G, 0, 1, 10), (G, 0, 0, 11), (G, 0, 1, 11), (TK, 1, 0), (ARR, 1),
    (A1, 2, 0, 0), (A1, 2, 1, 2), (TD, 1, 0), (TH, 0, 5), (G, 0, 1, 12), (G, 0, 0, 12), (TH, 0, 6), (A1, 2, 1, 1),
    (B2, 2, 1, 1), (TK, 1, 1), (B2, 2, 1, 0), (TD, 1, 1), (PR, 3, 0, 0), (B1, 3, 0), (A1, 3, 0, 0), (A1, 3, 1, 0),
    (PR, 3, 0, 1), (PR, 3, 0, 2), (ARH, 1), (A1, 3, 0, 2), (A2, 2, 1), (B1, 3, 1), (ARD, 1), (A1, 3, 1, 2),
    (TH, 0, 7), (ACC, 0, 0), (ARS, 2), (A1, 3, 1, 1), (PR, 2, 0, 3), (B2, 2, 0, 0), (ACC, 0, 1), (GR, 0), (CFIN, 0),
    (B2, 2, 0, 1), (A1, 2, 1, 3), (CFIN, 1), (A2, 3, 0), (B2, 3, 1, 1), (A1, 3, 0, 1), (B2, 3, 1, 0), (PR, 3, 0, 3),
    (A1, 2, 0, 2), (ARR, 2), (CW, 0), (G, 1, 0, 2), (G, 1, 0, 1), (G, 1, 0, 0), (CW, 1), (G, 1, 1, 1), (G, 1, 1, 2),
    (G, 1, 0, 3), (G, 1, 1, 0), (A2, 2, 0), (BP, 1), (ARS, 3), (G, 1, 0, 9), (B3, 3, 1), (G, 1, 0, 6), (G, 1, 0, 7),
    (A1, 3, 0, 3), (A1, 3, 1, 3), (TH, 1, 0), (G, 1, 0, 5), (A2, 3, 1), (G, 1, 1, 5), (G, 1, 0, 4), (A3, 2, 1, 0),
    (G, 1, 1, 3), (G, 1, 1, 6), (G, 1, 1, 7), (B3, 2, 1), (B2, 3, 0, 1), (ARR, 3), (G, 1, 0, 12), (G, 1, 1, 4),
    (A3, 2, 1, 1), (B2, 3, 0, 0), (A1, 2, 0, 3), (TH, 1, 1), (G, 1, 0, 11), (G, 1, 0, 10), (G, 1, 1, 9), (G, 1, 0, 8),
    (ARH, 2), (ARD, 2), (TH, 1, 2), (G, 1, 1, 8), (TH, 1, 3), (G, 1, 1, 11), (TH, 1, 4), (G, 1, 1, 10), (A3, 2, 0, 1),
    (G, 1, 1, 12), (A3, 2, 0, 0), (A3, 3, 1, 1), (B3, 2, 0), (B3, 3, 0), (A3, 3, 0, 0), (A3, 3, 1, 0), (ARH, 3),
    (A3, 3, 0, 1), (TH, 1, 5), (TH, 1, 6), (TH, 1, 7), (ACC, 1, 1), (ARD, 3), (FIN, 2, 1), (ACC, 1, 0), (GR, 1),
    (FIN, 2, 0), (FIN, 3, 1), (FIN, 3, 0), (END,),
)


def nn(a, b):
    return lax.dot_general(a, b, (((1,), (0,)), ((), ())), preferred_element_type=F32)


def nt(a, b):
    return lax.dot_general(a, b, (((1,), (1,)), ((), ())), preferred_element_type=F32)


def tn(a, b):
    return lax.dot_general(a, b, (((0,), (0,)), ((), ())), preferred_element_type=F32)


def mixed(first, second):
    return (MIX_WEIGHT * first.astype(F32) + (1.0 - MIX_WEIGHT) * second.astype(F32)).astype(BF)


def split(first, count, more):
    up = (count // 16 + more) // 2 * 16
    return pl.ds(first, up), pl.ds(first + up, count - up)


def scratch(tok, cb, rank):
    rows, wide = 2 * tok, 2 * cb
    forward = [n for halves in ROWS_LAST[0] + ROWS_OTHERS[0] for n in halves]
    na, nb = max(forward), tok - min(forward)
    ha, hb = (na // 16 + 1) // 2 * 16, (nb // 16 + 1) // 2 * 16
    piece = tok // NT
    vm = lambda *shape: pltpu.VMEM(shape, BF)
    vf = lambda *shape: pltpu.VMEM(shape, F32)
    dma = lambda *shape: pltpu.SemaphoreType.DMA(shape)
    table = dict(
        wb=vm(NX, NY, wide, cb),
        xin=vm(4, rows, wide),
        st=vm(2, tok, wide),
        sb=vm(2, rows, cb),
        tg=vm(2, rows, cb),
        dn=vm(wide, rank),
        do=vm(wide, rank),
        dr=vm(wide, rank),
        ur=vm(rank, cb),
        ax=vf(2, 8, tok),
        pb=vm(4, NX, NY, rows, cb),
        ra1=vm(4, HALVES, 4, na, cb),
        ra2=vm(4, HALVES, 2, ha, cb),
        ra3=vm(4, HALVES, 2, na, cb),
        rb1=vm(4, HALVES, 2, NX, hb, cb),
        rb2=vm(4, HALVES, 2, NX, nb, cb),
        rb3=vm(4, HALVES, nb, cb),
        po=vm(4, rows, cb),
        gb=vm(2, NX, NY, rows, cb),
        gx=vm(tok, cb),
        acc=vf(2, rows, wide),
        bs=vm(HALVES, tok, cb),
        br=vm(HALVES, tok, cb),
        es=vm(tok, wide),
        er=vm(tok, wide),
        co=vm(rows, cb),
        bps=vm(2, rows, rank),
        bpr=vm(2, tok, rank),
        hi=vf(2, HALVES, 2 * NT, 8, tok),
        ls=[vm(tok, parts * rank) for parts in (4, 1, 2, 1)],
        ai=[vm(NT, piece, parts * rank) for parts in (4, 1, 2, 1)],
        ao=[vm(rows, parts * rank) for parts in (4, 1, 2, 1)],
        l_sem=dma(21),
        e_sem=[dma(21), dma(21)],
        r_sem=[dma(4, HALVES, 13), dma(4, HALVES, 13)],
        g_sem=[dma(2, HALVES, 13), dma(2, HALVES, 13)],
        a_sem=[dma(4, 3), dma(4, 3)],
        h_sem=[dma(2, HALVES), dma(2, HALVES)],
        p_sem=[dma(3, HALVES), dma(3, HALVES)],
        m_sem=[dma(12), dma(12)],
    )
    return table


def kernel(
    tree,
    sections,
    width,
    base_weight,
    pol_down,
    pol_up,
    old_down,
    old_up,
    pol_in,
    ref_in,
    grad_in,
    stash,
    fresh_pol,
    fresh_ref,
    targets,
    final_gain,
    token_side,
    ref_logratio,
    pol_out,
    ref_out,
    grad_out,
    grad_down,
    grad_up,
    *buffers,
):
    b = SimpleNamespace(**jax.tree.unflatten(tree, buffers))
    wb, xin, pb, gb, acc = b.wb, b.xin, b.pb, b.gb, b.acc
    rows, wide = xin.shape[1:]
    tok, cb = rows // 2, wide // 2
    rank = pol_up.shape[1]
    piece = tok // NT

    s = lax.axis_index("section")
    t = lax.axis_index("tensor")
    c = lax.axis_index("dp")
    x, y = t // NY, t % NY
    ox, oc = 1 - x, 1 - c
    ring = [(y + i) % NY for i in range(NY)]
    order = (ring[2], ring[1], ring[3], ring[0])
    y1, y2, y3 = ring[1:]
    is_last = s == sections - 1
    is_first = s == 0
    pair = (s, t, oc)
    over = (s, ox * NY + y, c)
    ways = ((s, x * NY + y1, c), (s, x * NY + y3, c))
    near = (y1, y3)

    my_rows = pl.ds(pl.multiple_of(c * tok, tok), tok)
    its_rows = pl.ds(pl.multiple_of(oc * tok, tok), tok)
    my_cols = pl.ds(pl.multiple_of(c * cb, cb), cb)
    its_cols = pl.ds(pl.multiple_of(oc * cb, cb), cb)

    def half(h):
        return pl.ds(h * tok, tok)

    def size(part):
        return pl.ds(0, part.size)

    def inner(part, h):
        return pl.ds(part.start - h * tok, part.size)

    def f32(ref, *index):
        return ref[index].astype(F32)

    def send(src, dst, group, index, device):
        return pltpu.make_async_remote_copy(
            src_ref=src,
            dst_ref=dst,
            send_sem=group[0].at[index],
            recv_sem=group[1].at[index],
            device_id=device,
            device_id_type=MESH,
        )

    def weight_cols(xx, yy, core):
        first = pl.multiple_of((xx * NY + yy) * wide + core * cb, cb)
        return base_weight.at[0, :, pl.ds(first, cb)]

    own, away, place = {}, {}, {}
    for j in range(4):
        for side in range(2):
            xx, yy, name = (ox, x)[side], order[j], ("w", j, side)
            own[name] = (weight_cols(xx, yy, c), wb.at[xx, yy, my_cols, :])
            away[name] = (weight_cols(xx, yy, oc), wb.at[xx, yy, my_cols, :])

    def both(name, src, dst):
        own[name] = away[name] = (src, dst)

    def columns(name, src, dst):
        own[name] = (src.at[:, my_cols], dst)
        away[name] = (src.at[:, its_cols], dst)

    both("dn", pol_down.at[0], b.dn.at[my_cols])
    both("do", old_down.at[0], b.do.at[my_cols])
    both("p0", pol_in.at[0], xin.at[0, my_rows])
    both("r0", ref_in.at[0], xin.at[1, my_rows])
    both("fp", fresh_pol.at[0], xin.at[2, my_rows])
    both("fr", fresh_ref.at[0], xin.at[3, my_rows])
    columns("g0", grad_in.at[0], gb.at[0, x, y, my_rows])
    columns("s0", stash.at[0, 0], b.sb.at[0, my_rows])
    columns("s1", stash.at[0, 1], b.sb.at[1, my_rows])
    columns("t0", targets.at[0], b.tg.at[0, my_rows])
    columns("t1", targets.at[1], b.tg.at[1, my_rows])
    own["st"] = (stash.at[0], b.st)
    away["ax"] = (b.ax.at[c], b.ax.at[c])
    for name in list(own) + ["ax"]:
        place[name] = len(place)

    def local(name):
        return pltpu.make_async_copy(*own[name], b.l_sem.at[place[name]])

    def swap(name):
        return send(*away[name], b.e_sem, place[name], pair)

    weights = [("w", j, side) for j in range(4) for side in range(2)]
    for name in ["p0", *weights[:2], "dn", "do", "g0", "r0", "st", *weights[2:], "s0", "s1", "t0", "t1"]:
        local(name).start()

    @pl.when(is_first)
    def _():
        local("fp").start()
        local("fr").start()

    me = 2 * t + c
    barrier = pltpu.get_barrier_semaphore()

    def greet(d, _):
        other = (me + d) % (2 * NT)
        pl.semaphore_signal(barrier, inc=1, device_id=(s, other // 2, other % 2), device_id_type=MESH)
        return 0

    after = ((s + 1) % sections, t, c)
    before = ((s + sections - 1) % sections, t, c)
    lax.fori_loop(1, 2 * NT, greet, 0)
    pl.semaphore_signal(barrier, inc=1, device_id=after, device_id_type=MESH)
    pl.semaphore_signal(barrier, inc=1, device_id=before, device_id_type=MESH)
    pl.semaphore_wait(barrier, 2 * NT + 1)

    for name in ["p0", *weights[:2], "g0", "dn", "do", *weights[2:4], "r0", *weights[4:]]:
        swap(name).start()

    side = token_side[...]
    signs = (side == 1).astype(F32) - (side == 2).astype(F32)
    ratios = jnp.concatenate([jnp.broadcast_to(ref_logratio[:, k : k + 1], (1, tok)) for k in range(2)], axis=0)
    b.ax[c] = jnp.concatenate([signs, ratios, signs, ratios], axis=0)
    for name in ("ax", "t0", "s0", "s1", "t1"):
        swap(name).start()

    @pl.when(is_first)
    def _():
        swap("fp").start()
        swap("fr").start()

    def schedule(plan, forward_rows, backward_rows, last):
        seen, sent = set(), []

        def need(*wanted):
            for name in wanted:
                if name in seen:
                    continue
                seen.add(name)
                if isinstance(name, tuple) and name[0] == "g":
                    g_copy(*name[1:]).wait_recv()
                    continue
                if name != "ax":
                    local(name).wait()
                if name != "st":
                    swap(name).wait_recv()
                    sent.append(swap(name))

        def start(copy):
            copy.start()
            sent.append(copy)

        def part_rows(index):
            return pl.ds(pl.multiple_of(index * piece, piece), piece)

        here = pl.ds(pl.multiple_of(c * tok + t * piece, piece), piece)

        def ars(i):
            ls, ai = b.ls[i], b.ai[i]
            if i == 0:
                need("dn", "do", "p0", "r0", "st")
                b.dr[...] = mixed(b.dn[...], b.do[...])
                b.ur[...] = mixed(pol_up[0], old_up[0])
                terms = (
                    (xin.at[0, my_rows], b.dn),
                    (xin.at[1, my_rows], b.dr),
                    (b.st.at[0], b.dn),
                    (b.st.at[1], b.dn),
                )
            elif i == 2:
                terms = ((xin.at[2, my_rows], b.dn), (xin.at[3, my_rows], b.dr))
            else:
                k = i // 2
                send(b.bps.at[k, its_rows], b.bpr.at[k], b.m_sem, k, pair).wait_recv()
                ls[...] = (f32(b.bps, k, my_rows) + f32(b.bpr, k)).astype(BF)
                terms = ()
            for q, (ref, down) in enumerate(terms):
                ls[:, q * rank : (q + 1) * rank] = nn(ref[...], down[...]).astype(BF)

            def one(d, _):
                tt = (t + d) % NT
                send(ls.at[part_rows(tt)], ai.at[t], b.a_sem, (i, 0), (s, tt, c)).start()
                return 0

            lax.fori_loop(1, NT, one, 0)
            ai[t] = ls[part_rows(t)]

        def arr(i):
            ai, ao = b.ai[i], b.ao[i]
            seven = ai.at[pl.ds(0, NT - 1)]
            pltpu.make_async_copy(seven, seven, b.a_sem[1].at[i, 0]).wait()
            total = ai[0].astype(F32)
            for d in range(1, NT):
                total += ai[d].astype(F32)
            ao[here] = total.astype(BF)

            def one(d, _):
                tt = (t + d) % NT
                send(ao.at[here], ao.at[here], b.a_sem, (i, 1), (s, tt, c)).start()
                return 0

            lax.fori_loop(1, NT, one, 0)

        def arh(i):
            ao = b.ao[i]
            most = ao.at[pl.ds(0, piece * (NT - 1))]
            pltpu.make_async_copy(most, most, b.a_sem[1].at[i, 1]).wait()
            start(send(ao.at[my_rows], ao.at[my_rows], b.a_sem, (i, 2), pair))

        def ard(i):
            ao = b.ao[i]
            send(ao.at[my_rows], ao.at[my_rows], b.a_sem, (i, 2), pair).wait_recv()

        def sums_sent(i):
            seven = b.ai[i].at[pl.ds(0, NT - 1)]
            pltpu.make_async_copy(seven, seven, b.a_sem[0].at[i, 0]).wait()
            most = b.ao[i].at[pl.ds(0, piece * (NT - 1))]
            pltpu.make_async_copy(most, most, b.a_sem[0].at[i, 1]).wait()

        def a_part(p, h):
            return pl.ds(h * tok, forward_rows[p][h])

        def b_part(p, h):
            return pl.ds(h * tok + forward_rows[p][h], tok - forward_rows[p][h])

        def a_half(p, h, up):
            part = a_part(p, h)
            return split(part.start, part.size, 1)[up]

        def b_half(p, h, up):
            part = b_part(p, h)
            return split(part.start, part.size, 0)[up]

        def c_a1(p, h, j):
            part = a_part(p, h)
            return send(pb.at[p, ox, order[j], part], b.ra1.at[p, h, j, size(part)], b.r_sem, (p, h, j), over)

        def c_a2(p, h, up):
            part = a_half(p, h, up)
            return send(pb.at[p, x, y2, part], b.ra2.at[p, h, up, size(part)], b.r_sem, (p, h, 4 + up), ways[up])

        def c_b1(p, h, up):
            part = b_half(p, h, up)
            return send(pb.at[p, :, y2, part], b.rb1.at[p, h, up, :, size(part)], b.r_sem, (p, h, 6 + up), ways[up])

        def c_b2(p, h, up):
            part = b_part(p, h)
            return send(pb.at[p, :, near[up], part], b.rb2.at[p, h, up, :, size(part)], b.r_sem, (p, h, 8 + up), ways[up])

        def c_b3(p, h):
            part = b_part(p, h)
            return send(pb.at[p, ox, y, part], b.rb3.at[p, h, size(part)], b.r_sem, (p, h, 10), over)

        def c_a3(p, h, up):
            part = a_part(p, h)
            return send(pb.at[p, x, near[up], part], b.ra3.at[p, h, up, size(part)], b.r_sem, (p, h, 11 + up), ways[up])

        def pr(p, _, j):
            if p < 2:
                need(("p0", "r0")[p])
            need(("w", j, 0), ("w", j, 1))
            for xx in (ox, x):
                pb[p, xx, order[j]] = nn(xin[p], wb[xx, order[j]]).astype(BF)

        def a1(p, h, j):
            start(c_a1(p, h, j))

        def b1(p, h):
            start(c_b1(p, h, 0))
            start(c_b1(p, h, 1))

        def b2(p, h, up):
            part, yy = b_half(p, h, up), near[up]
            c_b1(p, h, up).wait_recv()
            for xx in range(NX):
                pb[p, xx, yy, part] = (f32(pb, p, xx, yy, part) + f32(b.rb1, p, h, up, xx, size(part))).astype(BF)
            start(c_b2(p, h, up))

        def a2(p, h):
            part = a_part(p, h)
            c_a1(p, h, 0).wait_recv()
            pb[p, x, y2, part] = (f32(pb, p, x, y2, part) + f32(b.ra1, p, h, 0, size(part))).astype(BF)
            start(c_a2(p, h, 0))
            start(c_a2(p, h, 1))

        def b3(p, h):
            part = b_part(p, h)
            n = size(part)
            c_b2(p, h, 0).wait_recv()
            c_b2(p, h, 1).wait_recv()
            pb[p, ox, y, part] = (
                f32(pb, p, ox, y, part) + f32(b.rb2, p, h, 0, ox, n) + f32(b.rb2, p, h, 1, ox, n)
            ).astype(BF)
            start(c_b3(p, h))

        def a3(p, h, up):
            yy, part, rest = near[up], a_half(p, h, up), a_half(p, h, 1 - up)
            c_a1(p, h, 1 + up).wait_recv()
            c_a2(p, h, up).wait_recv()
            pb[p, x, yy, part] = (
                f32(pb, p, x, yy, part)
                + f32(b.ra1, p, h, 1 + up, inner(part, h))
                + f32(b.ra2, p, h, up, size(part))
            ).astype(BF)
            pb[p, x, yy, rest] = (f32(pb, p, x, yy, rest) + f32(b.ra1, p, h, 1 + up, inner(rest, h))).astype(BF)
            start(c_a3(p, h, up))

        def fin(p, h):
            c_a1(p, h, 3).wait_recv()
            c_a3(p, h, 0).wait_recv()
            c_a3(p, h, 1).wait_recv()
            c_b3(p, h).wait_recv()
            low, up_ref = b.ao[p // 2 * 2], (pol_up[0], b.ur[...])[p % 2]
            low_cols = pl.ds(p % 2 * rank, rank)
            a, bb = a_part(p, h), b_part(p, h)
            na, nb = size(a), size(bb)
            summed = (
                f32(pb, p, x, y, a) + f32(b.ra1, p, h, 3, na) + f32(b.ra3, p, h, 0, na) + f32(b.ra3, p, h, 1, na),
                f32(pb, p, x, y, bb)
                + f32(b.rb2, p, h, 0, x, nb)
                + f32(b.rb2, p, h, 1, x, nb)
                + f32(b.rb3, p, h, nb),
            )
            for part, total in zip((a, bb), summed):
                adapted = ADAPTER_SCALE * nn(low[part, low_cols], up_ref)
                b.po[p, part] = (f32(xin, p, part, my_cols) + total + adapted).astype(BF)
            if p < 2:
                if not last:
                    start(c_pass(p, h))
                return
            out = (pol_out, ref_out)[p - 2]

            @pl.when(c == h)
            def _():
                out[0, :, my_cols] = b.po[p, half(h)]

            @pl.when(c != h)
            def _():
                c_out(p, h).start()

        def c_out(p, h):
            return send(b.po.at[p, half(h)], (pol_out, ref_out)[p - 2].at[0, :, my_cols], b.m_sem, p, pair)

        def c_pass(i, h):
            if i < 2:
                return send(b.po.at[i, half(h)], xin.at[2 + i, half(h), my_cols], b.p_sem, (i, h), after)
            return send(b.co.at[half(h)], gb.at[1, x, y, half(h)], b.p_sem, (2, h), before)

        def c_take(i, h):
            block = xin.at[2 + i, half(h), my_cols]
            return send(block, block, b.m_sem, 4 + 2 * i + h, pair)

        def unless_first(body):
            if last:
                body()
            else:
                pl.when(jnp.logical_not(is_first))(body)

        def tk(i, h):
            @unless_first
            def _():
                c_pass(i, h).wait_recv()
                c_take(i, h).start()

        def td(i, h):
            @unless_first
            def _():
                c_take(i, h).wait()

            if not last and ("fresh", i) not in seen:
                seen.add(("fresh", i))

                @pl.when(is_first)
                def _():
                    local(("fp", "fr")[i]).wait()
                    swap(("fp", "fr")[i]).wait()

        def hs(k, h):
            need(("t0", "t1")[k])
            p, part = 2 * k, half(h)
            gain = final_gain[:, my_cols]
            hidden = f32(b.po, p, part)
            squares = jnp.sum(hidden * hidden, axis=1, keepdims=True)
            inner_sum = jnp.sum(hidden * gain * f32(b.tg, k, part), axis=1, keepdims=True)
            lane = lax.broadcasted_iota(jnp.int32, (tok, 128), 1)
            b.hi[k, h, me] = jnp.where(lane == 0, squares, inner_sum).T[:8]

            def one(d, _):
                other = (me + d) % (2 * NT)
                slot = b.hi.at[k, h, me]
                send(slot, slot, b.h_sem, (k, h), (s, other // 2, other % 2)).start()
                return 0

            lax.fori_loop(1, 2 * NT, one, 0)

        def hw(k, h):
            if k == 0:
                need("g0")
            need("ax")
            others = b.hi.at[k, h, pl.ds(0, 2 * NT - 1)]
            pltpu.make_async_copy(others, others, b.h_sem[1].at[k, h]).wait()
            total = b.hi[k, h, 0]
            for d in range(1, 2 * NT):
                total += b.hi[k, h, d]
            sums = jnp.concatenate([total] * 16, axis=0).T
            squares, dot = sums[:, 0:1], sums[:, 1:2]
            r = lax.rsqrt(squares / width + NORM_EPSILON)
            aux = jnp.concatenate([b.ax[h]] * 16, axis=0).T
            sign, ratio = aux[:, k : k + 1], aux[0:1, 2 + k : 3 + k]
            margin = PREF_BETA * (jnp.sum(dot * r * sign, axis=0, keepdims=True) - ratio)
            weight = -LOSS_SCALE * PREF_BETA * jax.nn.sigmoid(-margin) * sign
            gain = final_gain[:, my_cols]
            hidden, target = f32(b.po, 2 * k, half(h)), f32(b.tg, k, half(h))
            g = weight * (r * gain * target - (dot * r * r * r / width) * hidden)
            gb[k, x, y, half(h)] = g.astype(BF)

        def head_sent(k, h):
            others = b.hi.at[k, h, pl.ds(0, 2 * NT - 1)]
            pltpu.make_async_copy(others, others, b.h_sem[0].at[k, h]).wait()

        routes = ((), (), (), (), (2,), (2,), (0,), (1,), (0,), (1,), (4,), (5,), (6, 7))

        def g_copy(k, h, i):
            n = backward_rows[k][h]
            first = h * tok
            a, bb = pl.ds(first, n), pl.ds(first + n, tok - n)
            low, high = split(first, tok, 0)
            a_low, a_high = split(first, n, 0)
            xx, yy, part, device = (
                (x, y, half(h), ways[0]),
                (x, y, half(h), ways[1]),
                (x, y, a, over),
                (x, y, bb, over),
                (ox, y, a, ways[0]),
                (ox, y, a, ways[1]),
                (x, y3, low, ways[0]),
                (x, y1, high, ways[1]),
                (x, y3, bb, over),
                (x, y1, bb, over),
                (ox, y3, a_low, ways[0]),
                (ox, y1, a_high, ways[1]),
                (x, y2, bb, over),
            )[i]
            block = gb.at[k, xx, yy, part]
            return send(block, block, b.g_sem, (k, h, i), device)

        def g(k, h, i):
            if k == 0 and not last:
                need("g0")
            need(*[("g", k, h, q) for q in routes[i]])
            start(g_copy(k, h, i))

        def th(k, q):
            need(*weights)
            if k == 0 and not last:
                need("g0")
            xx, yy, wanted = (
                (x, y, ()),
                (x, y3, (0,)),
                (x, y1, (1,)),
                (ox, y, (2, 3)),
                (x, y2, (6, 7)),
                (ox, y3, (4, 8)),
                (ox, y1, (5, 9)),
                (ox, y2, (10, 11, 12)),
            )[q]
            need(*[("g", k, h, i) for h in range(HALVES) for i in wanted])
            term = nt(gb[k, xx, yy], wb[xx, yy])
            acc[k] = term if q == 0 else acc[k] + term

        def c_acc(h):
            return send(b.bs.at[h], b.br.at[h], b.m_sem, 8 + h, pair)

        def c_end():
            return send(b.es, b.er, b.m_sem, 10, pair)

        def c_gx():
            return send(gb.at[1, x, y, its_rows], b.gx, b.m_sem, 11, pair)

        def acc_(k, h):
            if k == 0:
                b.bs[h] = acc[0, half(h), its_cols].astype(BF)
                start(c_acc(h))
            else:

                @pl.when(c != h)
                def _():
                    b.es[...] = acc[1, half(h)].astype(BF)
                    c_end().start()

        def bp(k):
            if k == 0 and not last:
                need("g0")
            b.bps[k] = nt(gb[k, x, y], pol_up[0]).astype(BF)
            start(send(b.bps.at[k, its_rows], b.bpr.at[k], b.m_sem, k, pair))
            if k == 1:
                start(c_gx())

        def cfin(h):
            c_acc(h).wait_recv()
            back = b.ao[1][half(h)]
            adapted = ADAPTER_SCALE * nt(back, b.dn[my_cols])
            total = f32(gb, 0, x, y, half(h)) + acc[0, half(h), my_cols] + f32(b.br, h)
            b.co[half(h)] = (total + adapted).astype(BF)
            if last:
                start(c_pass(2, h))
            else:

                @pl.when(jnp.logical_not(is_first))
                def _():
                    c_pass(2, h).start()

        def cw(h):
            c_pass(2, h).wait_recv()

        def gr(k):
            need("s0", "s1")
            back = b.ao[2 * k + 1][...]
            if last:
                stored, low = xin[2 * k, :, my_cols], b.ao[2 * k][:, 0:rank]
            else:
                stored, low = b.sb[k], b.ao[0][:, (2 + k) * rank : (3 + k) * rank]
            down = ADAPTER_SCALE * tn(stored, back)
            up = ADAPTER_SCALE * tn(low, gb[k, x, y])
            if k == 0:
                grad_down[0] = down
                grad_up[0] = up
            else:
                grad_down[0] += down
                grad_up[0] += up

        def end():
            c_gx().wait_recv()
            c_end().wait_recv()
            back = b.ao[3][my_rows]
            for cols, cotangent in ((my_cols, gb.at[1, x, y, my_rows]), (its_cols, b.gx)):
                adapted = ADAPTER_SCALE * nt(back, b.dn[cols])
                total = cotangent[...].astype(F32) + acc[1, my_rows, cols] + b.er[:, cols].astype(F32)
                grad_out[0, :, cols] = (total + adapted).astype(BF)
            need(*[name for name in place if name not in ("fp", "fr")])
            for p in (2, 3):
                c_out(p, 0).wait()
            c_end().wait_send()
            for copy in sent:
                copy.wait_send()
            if not last:

                @unless_first
                def _():
                    for h in range(HALVES):
                        c_pass(2, h).wait_send()

            for i in range(4):
                sums_sent(i)
            if last:
                for k in range(2):
                    for h in range(HALVES):
                        head_sent(k, h)

        steps = (
            pr, a1, a2, a3, b1, b2, b3, fin, ars, arr, arh, ard, hs, hw, g, th, bp, acc_, cfin, cw, tk, td, gr, end
        )
        for step, *index in plan:
            steps[step](*index)

    @pl.when(is_last)
    def _():
        schedule(PLAN_LAST, *ROWS_LAST, True)

    @pl.when(jnp.logical_not(is_last))
    def _():
        schedule(PLAN_OTHERS, *ROWS_OTHERS, False)


def put(*refs):
    copies = [pltpu.make_async_copy(refs[i], refs[5 + i], refs[10].at[i]) for i in range(5)]
    for copy in copies:
        copy.start()
    for copy in copies:
        copy.wait()


def on_device(sections, width, *operands):
    pol_in = operands[5]
    tok, wide = pol_in.shape[1:]
    cb = wide // 2
    rank = operands[1].shape[2]
    operands = list(operands)
    operands[12] = operands[12].reshape(1, wide)
    operands[14] = operands[14].reshape(1, 2)
    buffers, tree = jax.tree.flatten(scratch(tok, cb, rank))
    anywhere = pl.BlockSpec(memory_space=pl.ANY)
    inside = pl.BlockSpec(memory_space=pltpu.VMEM)
    in_vmem = (2, 4, 12, 13, 14)
    outs = (
        jax.ShapeDtypeStruct((1, tok, wide), BF),
        jax.ShapeDtypeStruct((1, tok, wide), BF),
        jax.ShapeDtypeStruct((1, tok, wide), BF),
        jax.ShapeDtypeStruct((1, cb, rank), F32),
        jax.ShapeDtypeStruct((1, rank, cb), F32),
    )
    results = pl.pallas_call(
        functools.partial(kernel, tree, sections, width),
        out_shape=outs,
        in_specs=[inside if i in in_vmem else anywhere for i in range(15)],
        out_specs=[inside] * 5,
        scratch_shapes=buffers,
        compiler_params=pltpu.CompilerParams(
            collective_id=0, has_side_effects=True, vmem_limit_bytes=56 * 1024 * 1024
        ),
        name="relay",
    )(*operands)
    return pl.pallas_call(
        put,
        out_shape=outs,
        in_specs=[inside] * 5,
        out_specs=[anywhere] * 5,
        scratch_shapes=[pltpu.SemaphoreType.DMA((5,))],
        name="put",
    )(*results)


def solution(mesh):
    in_specs = (
        P("section", ("tensor", "dp"), None),
        P("section", ("tensor", "dp"), None),
        P("section", None, ("tensor", "dp")),
        P("section", ("tensor", "dp"), None),
        P("section", None, ("tensor", "dp")),
        P("section", "dp", "tensor"),
        P("section", "dp", "tensor"),
        P("section", "dp", "tensor"),
        P("section", None, "dp", "tensor"),
        P(None, "dp", "tensor"),
        P(None, "dp", "tensor"),
        P(None, "dp", "tensor"),
        P("tensor"),
        P(None, "dp"),
        P(None, "dp"),
    )
    out_specs = (
        P("section", "dp", "tensor"),
        P("section", "dp", "tensor"),
        P("section", "dp", "tensor"),
        P("section", ("tensor", "dp"), None),
        P("section", None, ("tensor", "dp")),
    )
    sections = mesh.shape["section"]

    def whole(base_weight, *rest):
        body = functools.partial(on_device, sections, base_weight.shape[1])
        return jax.shard_map(
            body, mesh=mesh, in_specs=in_specs, out_specs=out_specs, check_vma=False
        )(base_weight, *rest)

    return whole
```

time: 504 us -> 123 us (0.24)
  blocking collectives: 315 us -> 0 us
  Pallas kernels: 0 us -> 122 us
  waiting for transfers between devices: 84.5 us -> 0 us
  matrix products: 60.1 us -> 0 us
  between operations: 17.3 us -> 0.87 us
  local copies, waits for them, and re-layouts: 15.6 us -> 0 us
  starting transfers between devices: 5.73 us -> 0 us
    psum x5 -> x0, blocking collectives: 227 us -> none  [the longest x4 213 us: on_device(): lax.psum((jnp.dot(pol_rows, policy_down, preferred_element_type=jnp.float...]
    pallas_call x0 -> x2, Pallas kernels: none -> 122 us  [the longest x1 119 us: on_device(): pl.pallas_call(functools.partial(kernel, tree, sections, width), out_shap...]
    all_to_all x14 -> x0, blocking collectives: 87.6 us -> none  [the longest x2 15.8 us: on_device(): lax.all_to_all(result, 'dp', split_axis=0, concat_axis=1, tiled=True)]
    dot_general x24 -> x0, matrix products: 60.1 us -> none  [the longest x2 18 us: on_device(): jnp.dot(ref_rows, weight, preferred_element_type=jnp.float32)]
    reduce_scatter x4 -> x0, waiting for transfers between devices: 55 us -> none  [the longest x2 37.5 us: on_device(): lax.psum_scatter(jnp.dot(pol_rows, weight, preferred_element_type=jnp.flo...]
    ppermute x3 -> x0, waiting for transfers between devices: 29.3 us -> none  [passed_along(): return lax.ppermute(block, axis, route)]
    ppermute x3 -> x0, starting transfers between devices: 5.48 us -> none  [passed_along(): return lax.ppermute(block, axis, route)]
  transfers between devices with their start and end apart: 9 -> 0, of which waited for: 7 -> 0; matrix products, arithmetic and copies ran while one was open for 9% -> 0% of each run, Pallas kernels for 0% -> 0%
where the time goes in v2:
time: 123 us; the launch traced here: 122 us
  Pallas kernels  122 us (99%)
    pallas_call x1, Pallas kernels, on_device(): pl.pallas_call(functools.partial(kernel, tree, sections, width), out_shap...  119 us

profile of v2, /device:TPU:229, one launch (start us, length us, event | category | flops | bytes accessed | tf_op | source)
XLA Modules:
  0.0 122.5 jit_solution(7924882621503604082)
XLA Ops:
  0.6 119.2 %relay.1 = (bf16[1,128,1024]{2,1,0:T(8,128)(2,1)}, bf16[1,128,1024]{2,1,0:T(8,128)(2,1)}, bf16[1,128,1024]{2,1,0:T(8,128)(2,1)}, f32[1,512,128]{2,1,0:T(8,128)}, f32[1,128,512]{2,1,0:T(8,128)}) custom-call(bf16[1,512,8192]{2,1,0:T(8,128)(2,1)} %base_weight.1, bf16[1,512,128]{2,1,0:T(8,128)(2,1)} %pol_down.1, bf16[1,128,512]{2,1,0:T(8,128)(2,1)} %pol_up.1, ...), custom_call_target="tpu_custom_call" | custom-call | tf_op jit(solution)/shard_map/relay/pallas_call | solution.py:788
  119.9 2.4 %put.1 = (bf16[1,128,1024]{2,1,0:T(8,128)(2,1)}, bf16[1,128,1024]{2,1,0:T(8,128)(2,1)}, bf16[1,128,1024]{2,1,0:T(8,128)(2,1)}, f32[1,512,128]{2,1,0:T(8,128)}, f32[1,128,512]{2,1,0:T(8,128)}) custom-call(bf16[1,128,1024]{2,1,0:T(8,128)(2,1)} %get-tuple-element.10.refs_0_, bf16[1,128,1024]{2,1,0:T(8,128)(2,1)} %get-tuple-element.11.refs_1_, ...), custom_call_target="tpu_custom_call" | custom-call | tf_op jit(solution)/shard_map/put/pallas_call | solution.py:799

commit v3 on v2

--- a/solution.py
+++ b/solution.py
@@ -15,7 +15,7 @@
 NX, NY = 2, 4
 NT = NX * NY
 HALVES = 2
-ROWS_LAST = (((48, 80), (64, 48), (32, 80), (48, 48)), ((96, 96), (64, 112)))
+ROWS_LAST = (((48, 64), (80, 48), (32, 64), (32, 48)), ((80, 80), (64, 96)))
 ROWS_OTHERS = (((32, 64), (48, 32), (64, 32), (48, 48)), ((112, 80), (80, 96)))
 
 ADAPTER_SCALE = 0.5
@@ -26,34 +26,34 @@
 
 PR, A1, A2, A3, B1, B2, B3, FIN, ARS, ARR, ARH, ARD,     HS, HW, G, TH, BP, ACC, CFIN, CW, TK, TD, GR, END = range(24)
 PLAN_LAST = (
-    (PR, 0, 0, 0), (B1, 0, 0), (A1, 0, 0, 0), (B1, 0, 1), (A1, 0, 1, 0), (ARS, 0), (PR, 0, 0, 1), (A1, 0, 0, 1),
-    (A2, 0, 0), (A1, 0, 1, 1), (B2, 0, 0, 0), (PR, 0, 0, 2), (B2, 0, 0, 1), (A2, 0, 1), (A1, 0, 1, 2), (PR, 1, 0, 0),
-    (B1, 1, 0), (B2, 0, 1, 1), (A1, 0, 0, 2), (PR, 0, 0, 3), (A1, 1, 1, 0), (ARR, 0), (B2, 0, 1, 0), (B1, 1, 1),
-    (A1, 0, 1, 3), (A3, 0, 1, 1), (B3, 0, 0), (PR, 1, 0, 1), (PR, 1, 0, 2), (A3, 0, 1, 0), (A1, 0, 0, 3),
-    (PR, 1, 0, 3), (B3, 0, 1), (A1, 1, 1, 1), (A3, 0, 0, 0), (A3, 0, 0, 1), (B2, 1, 0, 1), (A1, 1, 0, 0), (ARH, 0),
-    (B2, 1, 1, 0), (ARD, 0), (A1, 1, 1, 2), (FIN, 0, 1), (HS, 0, 1), (A2, 1, 1), (FIN, 0, 0), (HS, 0, 0),
-    (B2, 1, 1, 1), (A1, 1, 0, 2), (A1, 1, 0, 1), (B2, 1, 0, 0), (A2, 1, 0), (A1, 1, 1, 3), (HW, 0, 1), (A1, 1, 0, 3),
-    (G, 0, 1, 0), (G, 0, 1, 2), (G, 0, 1, 1), (HW, 0, 0), (G, 0, 0, 2), (BP, 0), (G, 0, 0, 0), (TH, 0, 0),
-    (G, 0, 0, 1), (G, 0, 1, 3), (ARS, 1), (B3, 1, 1), (G, 0, 1, 6), (A3, 1, 0, 1), (G, 0, 1, 7), (G, 0, 0, 3),
-    (G, 0, 1, 8), (A3, 1, 0, 0), (G, 0, 0, 4), (TK, 0, 0), (G, 0, 0, 8), (G, 0, 0, 9), (G, 0, 0, 7), (TH, 0, 1),
-    (A3, 1, 1, 1), (TD, 0, 0), (G, 0, 1, 5), (G, 0, 1, 9), (G, 0, 0, 6), (B3, 1, 0), (G, 0, 0, 5), (ARR, 1),
-    (G, 0, 1, 4), (A3, 1, 1, 0), (G, 0, 1, 12), (TK, 0, 1), (TD, 0, 1), (PR, 2, 0, 0), (A1, 2, 1, 0), (G, 0, 0, 12),
-    (B1, 2, 0), (PR, 2, 0, 1), (PR, 2, 0, 2), (G, 0, 1, 11), (A1, 2, 0, 0), (A1, 2, 0, 1), (PR, 2, 0, 3), (B1, 2, 1),
-    (G, 0, 0, 11), (G, 0, 0, 10), (A1, 2, 0, 2), (TH, 0, 2), (G, 0, 1, 10), (A1, 2, 1, 3), (ARH, 1), (FIN, 1, 1),
-    (A1, 2, 1, 1), (B2, 2, 0, 0), (B2, 2, 0, 1), (TH, 0, 3), (A2, 2, 1), (TH, 0, 4), (A1, 2, 1, 2), (FIN, 1, 0),
-    (TH, 0, 5), (A1, 2, 0, 3), (TK, 1, 0), (TH, 0, 6), (TH, 0, 7), (TD, 1, 0), (ARD, 1), (ACC, 0, 0), (CFIN, 0),
-    (B2, 2, 1, 0), (B2, 2, 1, 1), (TK, 1, 1), (ACC, 0, 1), (TD, 1, 1), (ARS, 2), (CFIN, 1), (A2, 2, 0), (PR, 3, 0, 0),
-    (B1, 3, 0), (A3, 2, 1, 0), (PR, 3, 0, 1), (A1, 3, 0, 1), (A3, 2, 1, 1), (ARR, 2), (B1, 3, 1), (B3, 2, 1),
-    (A3, 2, 0, 1), (A3, 2, 0, 0), (B3, 2, 0), (B2, 3, 0, 0), (PR, 3, 0, 2), (PR, 3, 0, 3), (A1, 3, 0, 2),
-    (B2, 3, 0, 1), (ARH, 2), (ARD, 2), (FIN, 2, 1), (HS, 1, 1), (A1, 3, 1, 1), (FIN, 2, 0), (HS, 1, 0), (B2, 3, 1, 0),
-    (A1, 3, 1, 2), (B2, 3, 1, 1), (A1, 3, 0, 0), (B3, 3, 0), (HW, 1, 1), (G, 1, 1, 0), (G, 1, 1, 1), (A1, 3, 1, 0),
-    (HW, 1, 0), (G, 1, 0, 0), (G, 1, 0, 1), (G, 1, 1, 2), (G, 1, 0, 2), (G, 1, 0, 3), (BP, 1), (GR, 0), (ARS, 3),
-    (G, 1, 1, 3), (B3, 3, 1), (A2, 3, 1), (G, 1, 1, 7), (G, 1, 1, 6), (G, 1, 1, 4), (G, 1, 1, 5), (G, 1, 0, 6),
-    (TH, 1, 0), (G, 1, 0, 4), (G, 1, 0, 9), (TH, 1, 1), (G, 1, 0, 8), (TH, 1, 2), (G, 1, 0, 7), (A1, 3, 0, 3),
-    (G, 1, 1, 8), (TH, 1, 3), (G, 1, 0, 5), (G, 1, 1, 12), (A2, 3, 0), (ARR, 3), (A3, 3, 1, 0), (G, 1, 1, 9),
-    (G, 1, 1, 10), (G, 1, 1, 11), (G, 1, 0, 12), (G, 1, 0, 11), (A1, 3, 1, 3), (G, 1, 0, 10), (TH, 1, 4),
-    (A3, 3, 1, 1), (A3, 3, 0, 1), (A3, 3, 0, 0), (ARH, 3), (TH, 1, 5), (TH, 1, 6), (TH, 1, 7), (ACC, 1, 1),
-    (ACC, 1, 0), (ARD, 3), (GR, 1), (FIN, 3, 0), (FIN, 3, 1), (END,),
+    (PR, 0, 0, 0), (B1, 0, 0), (A1, 0, 1, 0), (A1, 0, 0, 0), (ARS, 0), (B1, 0, 1), (PR, 0, 0, 1), (A1, 0, 0, 1),
+    (PR, 1, 0, 0), (A1, 1, 1, 0), (B1, 1, 1), (PR, 0, 0, 2), (A1, 0, 1, 1), (B2, 0, 0, 1), (A2, 0, 1), (PR, 1, 0, 1),
+    (A1, 1, 1, 1), (A2, 0, 0), (B2, 0, 0, 0), (B2, 0, 1, 1), (PR, 0, 0, 3), (A1, 0, 1, 2), (A1, 0, 0, 2),
+    (A1, 0, 0, 3), (B2, 0, 1, 0), (ARR, 0), (PR, 1, 0, 2), (B1, 1, 0), (A3, 0, 1, 0), (A1, 1, 1, 2), (A1, 1, 0, 0),
+    (A3, 0, 0, 0), (A2, 1, 1), (B3, 0, 0), (PR, 1, 0, 3), (A1, 0, 1, 3), (B2, 1, 1, 0), (B3, 0, 1), (A3, 0, 0, 1),
+    (A3, 0, 1, 1), (B2, 1, 0, 1), (ARH, 0), (A1, 1, 0, 2), (A3, 1, 1, 1), (ARD, 0), (FIN, 0, 0), (HS, 0, 0),
+    (A2, 1, 0), (A1, 1, 1, 3), (FIN, 0, 1), (HS, 0, 1), (A3, 1, 1, 0), (B2, 1, 1, 1), (A1, 1, 0, 3), (B2, 1, 0, 0),
+    (A1, 1, 0, 1), (HW, 0, 0), (G, 0, 0, 0), (G, 0, 0, 2), (A3, 1, 0, 1), (HW, 0, 1), (G, 0, 1, 3), (G, 0, 1, 1),
+    (TH, 0, 0), (BP, 0), (G, 0, 1, 2), (G, 0, 1, 0), (G, 0, 0, 1), (ARS, 1), (A3, 1, 0, 0), (B3, 1, 0), (G, 0, 0, 3),
+    (G, 0, 0, 4), (TK, 0, 0), (G, 0, 0, 5), (G, 0, 1, 9), (TH, 0, 1), (G, 0, 1, 7), (B3, 1, 1), (G, 0, 1, 4),
+    (G, 0, 1, 6), (G, 0, 1, 8), (G, 0, 0, 9), (G, 0, 1, 5), (TK, 0, 1), (G, 0, 0, 7), (FIN, 1, 0), (G, 0, 0, 8),
+    (TH, 0, 2), (TD, 0, 1), (TD, 0, 0), (ARR, 1), (G, 0, 0, 6), (PR, 2, 0, 0), (B1, 2, 0), (PR, 2, 0, 1),
+    (A1, 2, 1, 0), (A1, 2, 0, 0), (B1, 2, 1), (G, 0, 1, 12), (PR, 2, 0, 2), (G, 0, 1, 11), (TH, 0, 3), (PR, 2, 0, 3),
+    (A1, 2, 0, 3), (G, 0, 0, 10), (G, 0, 0, 12), (A1, 2, 1, 2), (G, 0, 0, 11), (G, 0, 1, 10), (A1, 2, 0, 2),
+    (TH, 0, 4), (A1, 2, 1, 3), (B2, 2, 0, 0), (ARH, 1), (A1, 2, 1, 1), (B2, 2, 0, 1), (TH, 0, 5), (B2, 2, 1, 1),
+    (TH, 0, 6), (ARD, 1), (FIN, 1, 1), (TK, 1, 0), (TD, 1, 0), (B2, 2, 1, 0), (TH, 0, 7), (ACC, 0, 0), (ACC, 0, 1),
+    (TK, 1, 1), (CFIN, 0), (TD, 1, 1), (ARS, 2), (GR, 0), (A2, 2, 0), (A1, 2, 0, 1), (A2, 2, 1), (PR, 3, 0, 0),
+    (CFIN, 1), (B1, 3, 0), (PR, 3, 0, 1), (B1, 3, 1), (ARR, 2), (A3, 2, 1, 1), (B3, 2, 1), (B3, 2, 0), (A3, 2, 1, 0),
+    (A3, 2, 0, 0), (A1, 3, 0, 0), (A1, 3, 1, 0), (A3, 2, 0, 1), (PR, 3, 0, 2), (PR, 3, 0, 3), (B2, 3, 0, 0),
+    (B2, 3, 0, 1), (ARH, 2), (A1, 3, 0, 3), (ARD, 2), (FIN, 2, 1), (HS, 1, 1), (FIN, 2, 0), (A1, 3, 0, 2), (HS, 1, 0),
+    (B2, 3, 1, 0), (A1, 3, 1, 3), (A2, 3, 0), (A1, 3, 1, 2), (B2, 3, 1, 1), (A1, 3, 1, 1), (A1, 3, 0, 1), (HW, 1, 1),
+    (G, 1, 1, 0), (G, 1, 1, 2), (G, 1, 1, 1), (HW, 1, 0), (BP, 1), (G, 1, 0, 1), (G, 1, 0, 3), (TH, 1, 0),
+    (G, 1, 1, 3), (G, 1, 0, 0), (G, 1, 0, 2), (ARS, 3), (B3, 3, 0), (G, 1, 1, 5), (G, 1, 1, 4), (G, 1, 1, 6),
+    (G, 1, 1, 7), (G, 1, 1, 8), (G, 1, 1, 9), (G, 1, 0, 6), (G, 1, 0, 9), (G, 1, 0, 8), (TH, 1, 1), (G, 1, 0, 4),
+    (G, 1, 0, 7), (G, 1, 0, 5), (ARR, 3), (TH, 1, 2), (G, 1, 1, 12), (A2, 3, 1), (G, 1, 1, 11), (TH, 1, 3),
+    (G, 1, 1, 10), (G, 1, 0, 12), (A3, 3, 0, 0), (TH, 1, 4), (G, 1, 0, 11), (G, 1, 0, 10), (B3, 3, 1), (TH, 1, 5),
+    (A3, 3, 0, 1), (A3, 3, 1, 1), (ARH, 3), (A3, 3, 1, 0), (TH, 1, 6), (ARD, 3), (TH, 1, 7), (ACC, 1, 1), (ACC, 1, 0),
+    (FIN, 3, 0), (GR, 1), (FIN, 3, 1), (END,),
 )
 PLAN_OTHERS = (
     (G, 0, 0, 0), (G, 0, 0, 2), (G, 0, 0, 1), (G, 0, 1, 3), (PR, 0, 0, 0), (B1, 0, 0), (B1, 0, 1), (PR, 0, 0, 1),
@@ -125,6 +125,8 @@
         dn=vm(wide, rank),
         do=vm(wide, rank),
         dr=vm(wide, rank),
+        up=vm(rank, cb),
+        ou=vm(rank, cb),
         ur=vm(rank, cb),
         ax=vf(2, 8, tok),
         pb=vm(4, NX, NY, rows, cb),
@@ -149,8 +151,8 @@
         ls=[vm(tok, parts * rank) for parts in (4, 1, 2, 1)],
         ai=[vm(NT, piece, parts * rank) for parts in (4, 1, 2, 1)],
         ao=[vm(rows, parts * rank) for parts in (4, 1, 2, 1)],
-        l_sem=dma(21),
-        e_sem=[dma(21), dma(21)],
+        l_sem=dma(23),
+        e_sem=[dma(23), dma(23)],
         r_sem=[dma(4, HALVES, 13), dma(4, HALVES, 13)],
         g_sem=[dma(2, HALVES, 13), dma(2, HALVES, 13)],
         a_sem=[dma(4, 3), dma(4, 3)],
@@ -266,6 +268,8 @@
     columns("t0", targets.at[0], b.tg.at[0, my_rows])
     columns("t1", targets.at[1], b.tg.at[1, my_rows])
     own["st"] = (stash.at[0], b.st)
+    own["up"] = (pol_up.at[0], b.up)
+    own["ou"] = (old_up.at[0], b.ou)
     away["ax"] = (b.ax.at[c], b.ax.at[c])
     for name in list(own) + ["ax"]:
         place[name] = len(place)
@@ -277,7 +281,7 @@
         return send(*away[name], b.e_sem, place[name], pair)
 
     weights = [("w", j, side) for j in range(4) for side in range(2)]
-    for name in ["p0", *weights[:2], "dn", "do", "g0", "r0", "st", *weights[2:], "s0", "s1", "t0", "t1"]:
+    for name in ["p0", *weights[:2], "dn", "do", "g0", "up", "ou", "r0", "st", *weights[2:], "s0", "s1", "t0", "t1"]:
         local(name).start()
 
     @pl.when(is_first)
@@ -328,7 +332,7 @@
                     continue
                 if name != "ax":
                     local(name).wait()
-                if name != "st":
+                if name in away:
                     swap(name).wait_recv()
                     sent.append(swap(name))
 
@@ -344,9 +348,9 @@
         def ars(i):
             ls, ai = b.ls[i], b.ai[i]
             if i == 0:
-                need("dn", "do", "p0", "r0", "st")
+                need("dn", "do", "p0", "r0", "st", "up", "ou")
                 b.dr[...] = mixed(b.dn[...], b.do[...])
-                b.ur[...] = mixed(pol_up[0], old_up[0])
+                b.ur[...] = mixed(b.up[...], b.ou[...])
                 terms = (
                     (xin.at[0, my_rows], b.dn),
                     (xin.at[1, my_rows], b.dr),
@@ -496,7 +500,7 @@
             c_a3(p, h, 0).wait_recv()
             c_a3(p, h, 1).wait_recv()
             c_b3(p, h).wait_recv()
-            low, up_ref = b.ao[p // 2 * 2], (pol_up[0], b.ur[...])[p % 2]
+            low, up_ref = b.ao[p // 2 * 2], (b.up, b.ur)[p % 2][...]
             low_cols = pl.ds(p % 2 * rank, rank)
             a, bb = a_part(p, h), b_part(p, h)
             na, nb = size(a), size(bb)
@@ -675,9 +679,10 @@
                     c_end().start()
 
         def bp(k):
+            need("up")
             if k == 0 and not last:
                 need("g0")
-            b.bps[k] = nt(gb[k, x, y], pol_up[0]).astype(BF)
+            b.bps[k] = nt(gb[k, x, y], b.up[...]).astype(BF)
             start(send(b.bps.at[k, its_rows], b.bpr.at[k], b.m_sem, k, pair))
             if k == 1:
                 start(c_gx())
@@ -777,7 +782,7 @@
     buffers, tree = jax.tree.flatten(scratch(tok, cb, rank))
     anywhere = pl.BlockSpec(memory_space=pl.ANY)
     inside = pl.BlockSpec(memory_space=pltpu.VMEM)
-    in_vmem = (2, 4, 12, 13, 14)
+    in_vmem = (12, 13, 14)
     outs = (
         jax.ShapeDtypeStruct((1, tok, wide), BF),
         jax.ShapeDtypeStruct((1, tok, wide), BF),

time: 123 us -> 122 us (level)
  no operation moved by 1% of the time
where the time goes in v3:
time: 122 us
  Pallas kernels  121 us (99%)
    pallas_call x1, Pallas kernels, on_device(): pl.pallas_call(functools.partial(kernel, tree, sections, width), out_shap...  119 us

profile of v3, /device:TPU:229, one launch (start us, length us, event | category | flops | bytes accessed | tf_op | source)
XLA Modules:
  0.0 122.0 jit_solution(1945742529948310405)
XLA Ops:
  0.6 118.7 %relay.1 = (bf16[1,128,1024]{2,1,0:T(8,128)(2,1)}, bf16[1,128,1024]{2,1,0:T(8,128)(2,1)}, bf16[1,128,1024]{2,1,0:T(8,128)(2,1)}, f32[1,512,128]{2,1,0:T(8,128)}, f32[1,128,512]{2,1,0:T(8,128)}) custom-call(bf16[1,512,8192]{2,1,0:T(8,128)(2,1)} %base_weight.1, bf16[1,512,128]{2,1,0:T(8,128)(2,1)} %pol_down.1, bf16[1,128,512]{2,1,0:T(8,128)(2,1)} %pol_up.1, ...), custom_call_target="tpu_custom_call" | custom-call | tf_op jit(solution)/shard_map/relay/pallas_call | solution.py:793
  119.4 2.4 %put.1 = (bf16[1,128,1024]{2,1,0:T(8,128)(2,1)}, bf16[1,128,1024]{2,1,0:T(8,128)(2,1)}, bf16[1,128,1024]{2,1,0:T(8,128)(2,1)}, f32[1,512,128]{2,1,0:T(8,128)}, f32[1,128,512]{2,1,0:T(8,128)}) custom-call(bf16[1,128,1024]{2,1,0:T(8,128)(2,1)} %get-tuple-element.10.refs_0_, bf16[1,128,1024]{2,1,0:T(8,128)(2,1)} %get-tuple-element.11.refs_1_, ...), custom_call_target="tpu_custom_call" | custom-call | tf_op jit(solution)/shard_map/put/pallas_call | solution.py:804
